TPU v7x, 128 devices: a whole 4x4x4 slice. The times are simulated.
128 devices in a mesh: kc: 16 (over x_hi, z, core), ia: 8 (over x_lo, y).
Axes of the slice: x: 4 (x_hi: 2, x_lo: 2; x = x_hi * 2 + x_lo), y: 4, z: 4, core: 2. Of those that a mesh axis runs over, the one named last changes fastest.
Arguments:
- amplitudes: bfloat16 [32768, 32768], P('ia', 'kc'), may hold values from -0.03125 to 0.03125
- occupied_factors: bfloat16 [2048, 4096], P('kc'), may hold values from -0.1875 to 0.1875
- virtual_factors: bfloat16 [2048, 4096], P('kc', 'ia'), may hold values from -6 to 6
Outputs:
- residual: float32 [32768, 512], P('ia', 'kc')
All inputs are finite; a program needn't handle non-finite values.
Results may differ from a plain program's by a relative error of at most 0.0029.
Values may be sent and summed in bfloat16 or wider, within the bound.
No kernel may reach another device: no remote copies, remote signals or barrier semaphores. Data moves between devices by JAX's collectives and lax.ppermute only.
A program may use at most 128 MiB of HBM per device.

v0:
```python
import jax
import jax.numpy as jnp
from jax import lax
from jax.sharding import PartitionSpec as P

O = 64
V = 512
BW = 8


def per_device(amplitudes, occupied_factors, virtual_factors):
    k_per_device = O // lax.axis_size("kc")
    c_per_device = V // lax.axis_size("ia")
    summed = lax.psum_scatter(
        lax.dot_general(
            occupied_factors,
            virtual_factors,
            (((0,), (0,)), ((), ())),
            preferred_element_type=jnp.float32,
        ),
        "kc",
        scatter_dimension=0,
        tiled=True,
    )
    integrals = summed.astype(jnp.bfloat16)
    blocks = (
        integrals.reshape(k_per_device, O, c_per_device, BW)
        .transpose(0, 2, 1, 3)
        .reshape(k_per_device, c_per_device, O * BW)
    )
    local_rows = amplitudes.shape[0]
    amplitude_view = amplitudes.reshape(local_rows, k_per_device, V)
    partial_sums = lax.dot_general(
        amplitude_view,
        lax.all_gather(blocks, "ia", axis=1, tiled=True),
        (((1, 2), (0, 1)), ((), ())),
        preferred_element_type=jnp.float32,
    )
    return lax.psum_scatter(partial_sums, "kc", scatter_dimension=1, tiled=True)


def solution(mesh):
    placed = (P("ia", "kc"), P("kc", None), P("kc", "ia"))
    return jax.shard_map(
        per_device, mesh=mesh, in_specs=placed, out_specs=P("ia", "kc"), check_vma=False
    )
```

profile of v0, /device:TPU:1, one launch (start us, length us, event | category | flops | bytes accessed | tf_op | source)
XLA Modules:
  0.0 285.1 jit_solution(17885568947497332595)
XLA Ops:
  6.5 0.0 copy-start
  6.5 0.0 reduce-scatter.3.cloned.1.call-start
  6.5 1.2 copy-done
  7.8 5.4 %fusion.6 = f32[4096,512]{1,0:T(8,128)} fusion(bf16[128,4096]{1,0:T(8,128)(2,1)S(1)} %copy-done, bf16[128,512]{1,0:T(8,128)(2,1)} %param.5), kind=kOutput, calls=%fused_computation.4 | convolution fusion | flops 536870912 | bytes 9568256 | tf_op jit(solution)/shard_map/dot_general | solution.py:15
  13.2 0.0 reduce-scatter.3.cloned.1.call-update
  13.2 0.0 all-gather.2.cloned.1.call-start
  13.2 104.7 %reduce-scatter.3.cloned.1.call-done = f32[256,512]{1,0:T(8,128)} async-done(((f32[4096,512]{1,0:T(8,128)}), f32[256,512]{1,0:T(8,128)}) %reduce-scatter.3.cloned.1.call-update) | async-done | bytes 524304 | tf_op jit(solution)/shard_map/reduce_scatter | solution.py:14
  117.9 1.1 convert_element_type.3
  119.0 0.1 copy.6
  119.1 0.2 reshape.9
  119.4 0.7 copy.7
  120.1 0.9 copy.8
  121.0 0.0 all-gather.2.cloned.1.call-update
  121.0 0.0 reduce-scatter.5.cloned.1.call-start
  121.1 36.2 %all-gather.2.cloned.1.call-done = bf16[4,512,512]{2,1,0:T(8,128)(2,1)} async-done(((bf16[4,64,512]{2,1,0:T(8,128)(2,1)}), bf16[4,512,512]{2,1,0:T(8,128)(2,1)}) %all-gather.2.cloned.1.call-update) | async-done | bytes 2097168 | tf_op jit(solution)/shard_map/all_gather | solution.py:35
  157.3 15.2 %fusion.3 = f32[4096,512]{0,1:T(8,128)} fusion(bf16[4,512,512]{2,1,0:T(8,128)(2,1)} %all-gather.2.cloned.1.call-done, bf16[512,4,8,512]{3,2,1,0:T(8,128)(2,1)} %bitcast.19), kind=kOutput, calls=%fused_computation.3 | convolution fusion | flops 8589934592 | bytes 27262976 | tf_op jit(solution)/shard_map/dot_general | solution.py:33
  172.5 0.0 reduce-scatter.5.cloned.1.call-update
  172.5 106.0 %reduce-scatter.5.cloned.1.call-done = f32[4096,32]{0,1:T(8,128)} async-done(((f32[4096,512]{0,1:T(8,128)}), f32[4096,32]{0,1:T(8,128)}) %reduce-scatter.5.cloned.1.call-update) | async-done | bytes 524304 | tf_op jit(solution)/shard_map/reduce_scatter | solution.py:39
Async XLA Ops:
  6.5 1.2 copy-start
  6.5 111.4 %reduce-scatter.3.cloned.1.call-start = ((), (), s32[]{:S(2)}) async-start(), calls=%async_computation.2 | async-start | bytes 8912896 | tf_op jit(solution)/shard_map/reduce_scatter | solution.py:14
  13.2 144.1 %all-gather.2.cloned.1.call-start = ((), (), s32[]{:S(2)}) async-start(), calls=%async_computation.3 | async-start | bytes 2359296 | tf_op jit(solution)/shard_map/all_gather | solution.py:35
  121.0 157.5 %reduce-scatter.5.cloned.1.call-start = ((), (), s32[]{:S(2)}) async-start(), calls=%async_computation.4 | async-start | bytes 8912896 | tf_op jit(solution)/shard_map/reduce_scatter | solution.py:39
Sparse Core Ops, SparseCore 0:
  13.3 104.5 reduce-scatter.2
  121.1 36.1 all-gather.1
  172.6 105.8 reduce-scatter.4
where the time goes:
time: 286 us; the launch traced here: 285 us
  waiting for transfers between devices  247 us (86%)
  matrix products  20.6 us (7%)
  between operations  13.1 us (5%)
  local copies, waits for them, and re-layouts  3.23 us (1%)
    reduce_scatter x1, waiting for transfers between devices, per_device(): return lax.psum_scatter(partial_sums, 'kc', scatter_dimension=1, tiled=True)  106 us
    reduce_scatter x1, waiting for transfers between devices, per_device(): lax.psum_scatter(lax.dot_general(occupied_factors, virtual_factors, (((0,...  105 us
    all_gather x1, waiting for transfers between devices, per_device(): lax.all_gather(blocks, 'ia', axis=1, tiled=True)  36.2 us
    dot_general x1, matrix products, per_device(): lax.dot_general(amplitude_view, lax.all_gather(blocks, 'ia', axis=1, tile...  15.2 us
  transfers between devices with their start and end apart: 3, of which 3 were waited for; matrix products, arithmetic and copies ran while one was open for 0% of the time, Pallas kernels for 0%

commit v1 on v0

v1 whole, which is shorter than its diff:
```python
import functools

import jax
import jax.numpy as jnp
from jax import lax
from jax.experimental import pallas as pl
from jax.experimental.pallas import tpu as pltpu
from jax.sharding import PartitionSpec as P

O = 64
V = 512
BW = 8
F32 = jnp.float32
BF16 = jnp.bfloat16
MIB = 1 << 20


def block_kernel(core_ref, kept_ref, came_ref, out_ref):
    kj, cb = kept_ref.shape
    ks = kj // O
    cs = cb // BW
    rows = O * BW
    integrals = (kept_ref[...] + came_ref[...]).astype(BF16)
    source = lax.broadcasted_iota(jnp.int32, (cb, cb), 0)
    target = lax.broadcasted_iota(jnp.int32, (cb, cb), 1)
    move = jnp.where(source == (target % cs) * BW + target // cs, 1.0, 0.0).astype(BF16)
    by_b = jnp.dot(integrals, move, preferred_element_type=F32).astype(BF16)
    stacked = jnp.concatenate(
        [
            jnp.concatenate(
                [by_b[k * O : (k + 1) * O, b * cs : (b + 1) * cs] for b in range(BW)], axis=0
            )
            for k in range(ks)
        ],
        axis=1,
    )
    half = rows // 2
    target = lax.broadcasted_iota(jnp.int32, (rows, rows), 0)
    source = lax.broadcasted_iota(jnp.int32, (rows, rows), 1)
    core = (core_ref[0] + target // half) % 2
    within = target % half
    j = (within // 32) * 8 + core * 4 + (within % 32) // BW
    move = jnp.where(source == (within % BW) * O + j, 1.0, 0.0).astype(BF16)
    out_ref[...] = jnp.dot(move, stacked, preferred_element_type=F32).astype(BF16)


def cycle_blocks(core, kept, came):
    kj, cb = kept.shape
    return pl.pallas_call(
        block_kernel,
        out_shape=jax.ShapeDtypeStruct((O * BW, kj // O * (cb // BW)), BF16),
        in_specs=[
            pl.BlockSpec(memory_space=pltpu.SMEM),
            pl.BlockSpec(memory_space=pltpu.VMEM),
            pl.BlockSpec(memory_space=pltpu.VMEM),
        ],
        out_specs=pl.BlockSpec(memory_space=pltpu.VMEM),
        compiler_params=pltpu.CompilerParams(vmem_limit_bytes=24 * MIB),
        cost_estimate=pl.CostEstimate(flops=4 * 512 * 512 * 256, bytes_accessed=2 * MIB, transcendentals=0),
    )(core, kept, came)


def residual_kernel(blocks_ref, amplitudes_ref, kept_ref, sent_ref, joined):
    parts, rows, width = blocks_ref.shape
    ks = 4
    cs = width // ks

    @pl.when(pl.program_id(0) == 0)
    def _():
        for k in range(ks):
            for pair in range(parts // 2):
                at = k * parts * cs + pair * 2 * cs
                joined[:, at : at + 2 * cs] = jnp.concatenate(
                    [blocks_ref[2 * pair + i, :, k * cs : (k + 1) * cs] for i in range(2)], axis=1
                )

    total = lax.dot_general(
        joined[...], amplitudes_ref[...], (((1,), (1,)), ((), ())), preferred_element_type=F32
    )
    kept_ref[...] = total[: rows // 2]
    sent_ref[...] = total[rows // 2 :].astype(BF16)


def residual_partials(blocks, amplitudes, tile=512):
    parts, rows, width = blocks.shape
    local_rows, depth = amplitudes.shape
    return pl.pallas_call(
        residual_kernel,
        grid=(local_rows // tile,),
        out_shape=(
            jax.ShapeDtypeStruct((rows // 2, local_rows), F32),
            jax.ShapeDtypeStruct((rows // 2, local_rows), BF16),
        ),
        in_specs=[
            pl.BlockSpec((parts, rows, width), lambda m: (0, 0, 0)),
            pl.BlockSpec((tile, depth), lambda m: (m, 0)),
        ],
        out_specs=(
            pl.BlockSpec((rows // 2, tile), lambda m: (0, m)),
            pl.BlockSpec((rows // 2, tile), lambda m: (0, m)),
        ),
        scratch_shapes=[pltpu.VMEM((rows, depth), BF16)],
        compiler_params=pltpu.CompilerParams(vmem_limit_bytes=32 * MIB),
        cost_estimate=pl.CostEstimate(
            flops=2 * rows * local_rows * depth, bytes_accessed=24 * MIB, transcendentals=0
        ),
    )(blocks, amplitudes)


def per_device(amplitudes, occupied_factors, virtual_factors):
    kc_size = lax.axis_size("kc")
    ia_size = lax.axis_size("ia")
    chips = kc_size // 2
    core = lax.axis_index("kc") % 2
    same_core = [[2 * t + c for t in range(chips)] for c in range(2)]
    swap = [(i, i ^ 1) for i in range(kc_size)]
    depth, kj = occupied_factors.shape
    cb = virtual_factors.shape[1]

    payload = jnp.concatenate(
        [
            occupied_factors.reshape(depth, chips, kj // chips).transpose(1, 0, 2),
            jnp.broadcast_to(virtual_factors[None], (chips, depth, cb)),
        ],
        axis=1,
    )
    factors = lax.all_to_all(payload, "kc", 0, 0, axis_index_groups=same_core)
    occupied = factors[:, :depth].reshape(chips * depth, kj // chips)
    virtual = factors[:, depth:].reshape(chips * depth, cb)
    partial = lax.dot_general(
        occupied, virtual, (((0,), (0,)), ((), ())), preferred_element_type=F32
    ).reshape(2, kj // kc_size, cb)
    kept = lax.dynamic_index_in_dim(partial, core, 0, keepdims=False)
    came = lax.ppermute(lax.dynamic_index_in_dim(partial, 1 - core, 0, keepdims=False), "kc", swap)
    own = cycle_blocks(core[None], kept, came)

    blocks = lax.all_to_all(jnp.broadcast_to(own[None], (ia_size,) + own.shape), "ia", 0, 0)

    kept, sent = residual_partials(blocks, amplitudes)
    came = lax.ppermute(sent, "kc", swap)
    chip_sums = (kept + came.astype(F32)).astype(BF16)
    shares = lax.all_to_all(
        chip_sums.reshape(chips, O * BW // kc_size, -1), "kc", 0, 0, axis_index_groups=same_core
    )
    return jnp.sum(shares.astype(F32), axis=0).T


def solution(mesh):
    placed = (P("ia", "kc"), P("kc", None), P("kc", "ia"))
    return jax.shard_map(
        per_device, mesh=mesh, in_specs=placed, out_specs=P("ia", "kc"), check_vma=False
    )
```

time: 286 us -> 129 us (0.45)
  waiting for transfers between devices: 247 us -> 31.5 us
  blocking collectives: 0 us -> 61.4 us
  matrix products: 20.6 us -> 0.7 us
  Pallas kernels: 0 us -> 14.7 us
  between operations: 13.1 us -> 0.08 us
  starting transfers between devices: 0.09 us -> 11.9 us
    reduce_scatter x2 -> x0, waiting for transfers between devices: 211 us -> none  [the longest x1 106 us: per_device(): return lax.psum_scatter(partial_sums, 'kc', scatter_dimension=1, tiled=True)]
    all_to_all x0 -> x2, blocking collectives: none -> 61.4 us  [the longest x1 31.8 us: per_device(): lax.all_to_all(chip_sums.reshape(chips, O * BW // kc_size, -1), 'kc', 0,...]
    all_gather x1 -> x0, waiting for transfers between devices: 36.2 us -> none  [per_device(): lax.all_gather(blocks, 'ia', axis=1, tiled=True)]
    all_to_all x0 -> x1, waiting for transfers between devices: none -> 26.1 us  [per_device(): factors = lax.all_to_all(payload, 'kc', 0, 0, axis_index_groups=same_core)]
    dot_general x2 -> x1, matrix products: 20.6 us -> 0.7 us  [per_device(): lax.dot_general(occupied, virtual, (((0,), (0,)), ((), ())), preferred_el...]
    pallas_call x0 -> x2, Pallas kernels: none -> 14.7 us  [the longest x1 13.9 us: residual_partials(): pl.pallas_call(residual_kernel, grid=(local_rows // tile,), out_shape=(ja...]
    all_to_all x0 -> x1, starting transfers between devices: none -> 8.32 us  [per_device(): factors = lax.all_to_all(payload, 'kc', 0, 0, axis_index_groups=same_core)]
    ppermute x0 -> x2, waiting for transfers between devices: none -> 5.32 us  [the longest x1 3.79 us: per_device(): came = lax.ppermute(sent, 'kc', swap)]
where the time goes in v1:
time: 129 us; the launch traced here: 127 us
  blocking collectives  61.4 us (48%)
  waiting for transfers between devices  31.5 us (24%)
  Pallas kernels  14.7 us (11%)
  starting transfers between devices  11.9 us (9%)
  local copies, waits for them, and re-layouts  4.03 us (3%)
  other arithmetic  3.13 us (2%)
    all_to_all x1, blocking collectives, per_device(): lax.all_to_all(chip_sums.reshape(chips, O * BW // kc_size, -1), 'kc', 0,...  31.8 us
    all_to_all x1, blocking collectives, per_device(): lax.all_to_all(jnp.broadcast_to(own[None], (ia_size,) + own.shape), 'ia',...  29.7 us
    all_to_all x1, waiting for transfers between devices, per_device(): factors = lax.all_to_all(payload, 'kc', 0, 0, axis_index_groups=same_core)  26.1 us
    pallas_call x1, Pallas kernels, residual_partials(): pl.pallas_call(residual_kernel, grid=(local_rows // tile,), out_shape=(ja...  13.9 us
    all_to_all x1, starting transfers between devices, per_device(): factors = lax.all_to_all(payload, 'kc', 0, 0, axis_index_groups=same_core)  8.32 us
    ppermute x1, waiting for transfers between devices, per_device(): came = lax.ppermute(sent, 'kc', swap)  3.79 us
  transfers between devices with their start and end apart: 3, of which 3 were waited for; matrix products, arithmetic and copies ran while one was open for 0% of the time, Pallas kernels for 0%

profile of v1, /device:TPU:1, one launch (start us, length us, event | category | flops | bytes accessed | tf_op | source)
XLA Modules:
  0.0 127.4 jit_solution(9382015987562761565)
XLA Ops:
  0.0 0.0 copy-start.1
  0.0 1.3 %copy.8 = bf16[16,8,8,512]{3,2,0,1:T(8,128)(2,1)S(1)} copy(bf16[16,8,8,512]{3,2,1,0:T(8,128)(2,1)} %bitcast.26) | data formatting | bytes 2097152 | tf_op jit(solution)/shard_map/reshape | solution.py:122
  1.4 0.0 copy-done.1
  1.4 0.1 broadcast_in_dim.7
  1.5 1.5 %pad_maximum_fusion = bf16[8,256,512]{2,1,0:T(8,128)(2,1)} fusion(bf16[8,128,512]{2,1,0:T(8,128)(2,1)S(1)} %broadcast_in_dim.7, bf16[8,128,512]{2,1,0:T(8,128)(2,1)S(1)} %bitcast.25), kind=kLoop, calls=%fused_computation.2 | loop fusion | flops 4194304 | bytes 4194304 | tf_op jit(solution)/shard_map/concatenate | solution.py:120
  2.9 8.3 %all-to-all-start = ((bf16[8,256,512]{2,1,0:T(8,128)(2,1)}), bf16[8,256,512]{2,1,0:T(8,128)(2,1)S(1)}, u32[]{:S(2)}, u32[]{:S(2)}) async-start(bf16[8,256,512]{2,1,0:T(8,128)(2,1)} %pad_maximum_fusion), calls=%async_computation | async-start | bytes 4194304 | tf_op jit(solution)/shard_map/all_to_all | solution.py:127
  11.3 26.1 %all-to-all-done = bf16[8,256,512]{2,1,0:T(8,128)(2,1)S(1)} async-done(((bf16[8,256,512]{2,1,0:T(8,128)(2,1)}), bf16[8,256,512]{2,1,0:T(8,128)(2,1)S(1)}, u32[]{:S(2)}, u32[]{:S(2)}) %all-to-all-start) | async-done | bytes 2097184 | tf_op jit(solution)/shard_map/all_to_all | solution.py:127
  37.4 1.2 fusion
  38.6 0.0 copy-start
  38.6 0.5 copy.5
  39.1 0.7 copy-done
  39.8 0.7 fusion.1
  40.5 0.1 dynamic-slice_bitcast_fusion
  40.6 1.3 %collective-permute-start = (f32[256,512]{1,0:T(8,128)S(1)}, f32[256,512]{1,0:T(8,128)S(1)}, u32[]{:S(2)}, u32[]{:S(2)}) collective-permute-start(f32[256,512]{1,0:T(8,128)S(1)} %get-tuple-element.11), channel_id=1, source_target_pairs={{0,8},{8,0},{16,24},{24,16},{32,40},{40,32},{48,56},{56,48},{64,72... | collective-permute-start | bytes 1572872 | tf_op jit(solution)/shard_map/ppermute | solution.py:134
  41.9 1.5 %collective-permute-done.came_ref = f32[256,512]{1,0:T(8,128)S(1)} collective-permute-done((f32[256,512]{1,0:T(8,128)S(1)}, f32[256,512]{1,0:T(8,128)S(1)}, u32[]{:S(2)}, u32[]{:S(2)}) %collective-permute-start) | collective-permute-done | bytes 524320 | tf_op jit(solution)/shard_map/ppermute | solution.py:134
  43.4 0.8 shard_map.37
  44.3 0.1 broadcast_in_dim.8
  44.4 29.7 %all_to_all.15.blocks_ref = bf16[8,512,256]{2,1,0:T(8,128)(2,1)S(1)} all-to-all(bf16[8,512,256]{2,1,0:T(8,128)(2,1)S(1)} %broadcast_in_dim.8), channel_id=1, replica_groups=mesh['kc'=16,'ia'=8] {'ia'}, dimensions={0} | all-to-all | bytes 4194304 | tf_op jit(solution)/shard_map/all_to_all | solution.py:137
  74.1 13.9 %shard_map.38 = (f32[256,4096]{1,0:T(8,128)S(1)}, bf16[256,4096]{1,0:T(8,128)(2,1)S(1)}) custom-call(bf16[8,512,256]{2,1,0:T(8,128)(2,1)S(1)} %all_to_all.15.blocks_ref, bf16[4096,2048]{1,0:T(8,128)(2,1)} %amplitudes_ref.1), custom_call_target="tpu_custom_call" | custom-call | flops 8589934592 | bytes 25165824 | tf_op jit(solution)/shard_map/pallas_call | solution.py:87
  88.0 2.3 %collective-permute-start.1 = (bf16[256,4096]{1,0:T(8,128)(2,1)S(1)}, bf16[256,4096]{1,0:T(8,128)(2,1)S(1)}, u32[]{:S(2)}, u32[]{:S(2)}) collective-permute-start(bf16[256,4096]{1,0:T(8,128)(2,1)S(1)} %get-tuple-element.8), channel_id=1, source_target_pairs={{0,8},{8,0},{16,24},{24,16},{32,40},{40,32},{48,56},{56,48},{64,72... | collective-permute-start | bytes 6291464 | tf_op jit(solution)/shard_map/ppermute | solution.py:140
  90.2 3.8 %collective-permute-done.1 = bf16[256,4096]{1,0:T(8,128)(2,1)S(1)} collective-permute-done((bf16[256,4096]{1,0:T(8,128)(2,1)S(1)}, bf16[256,4096]{1,0:T(8,128)(2,1)S(1)}, u32[]{:S(2)}, u32[]{:S(2)}) %collective-permute-start.1) | collective-permute-done | bytes 2097184 | tf_op jit(solution)/shard_map/ppermute | solution.py:140
  94.0 0.5 add_convert_fusion
  94.6 31.8 %all_to_all.16 = bf16[8,32,4096]{2,1,0:T(8,128)(2,1)S(1)} all-to-all(bf16[8,32,4096]{2,1,0:T(8,128)(2,1)S(1)} %bitcast.23), channel_id=1, replica_groups={{0,16,32,48,64,80,96,112},{8,24,40,56,72,88,104,120},{1,17,33,49,65,81,..., dimensions={0} | all-to-all | bytes 4194304 | tf_op jit(solution)/shard_map/all_to_all | solution.py:142
  126.3 1.1 convert_reduce_fusion
Async XLA Ops:
  0.0 1.4 %copy-start.1 = (bf16[128,512]{1,0:T(8,128)(2,1)S(1)}, bf16[128,512]{1,0:T(8,128)(2,1)}, u32[]{:S(2)}) copy-start(bf16[128,512]{1,0:T(8,128)(2,1)} %param.5) | copy-start | bytes 393220
  2.9 34.5 %all-to-all-start = ((bf16[8,256,512]{2,1,0:T(8,128)(2,1)}), bf16[8,256,512]{2,1,0:T(8,128)(2,1)S(1)}, u32[]{:S(2)}, u32[]{:S(2)}) async-start(bf16[8,256,512]{2,1,0:T(8,128)(2,1)} %pad_maximum_fusion), calls=%async_computation | async-start | bytes 4194304 | tf_op jit(solution)/shard_map/all_to_all | solution.py:127
  38.6 1.2 copy-start
  40.6 2.8 %collective-permute-start = (f32[256,512]{1,0:T(8,128)S(1)}, f32[256,512]{1,0:T(8,128)S(1)}, u32[]{:S(2)}, u32[]{:S(2)}) collective-permute-start(f32[256,512]{1,0:T(8,128)S(1)} %get-tuple-element.11), channel_id=1, source_target_pairs={{0,8},{8,0},{16,24},{24,16},{32,40},{40,32},{48,56},{56,48},{64,72... | collective-permute-start | bytes 1572872 | tf_op jit(solution)/shard_map/ppermute | solution.py:134
  88.0 6.0 %collective-permute-start.1 = (bf16[256,4096]{1,0:T(8,128)(2,1)S(1)}, bf16[256,4096]{1,0:T(8,128)(2,1)S(1)}, u32[]{:S(2)}, u32[]{:S(2)}) collective-permute-start(bf16[256,4096]{1,0:T(8,128)(2,1)S(1)} %get-tuple-element.8), channel_id=1, source_target_pairs={{0,8},{8,0},{16,24},{24,16},{32,40},{40,32},{48,56},{56,48},{64,72... | collective-permute-start | bytes 6291464 | tf_op jit(solution)/shard_map/ppermute | solution.py:140

commit v2 on v0

v2 whole, which is shorter than its diff:
```python
import functools

import jax
import jax.numpy as jnp
from jax import lax
from jax.experimental import pallas as pl
from jax.experimental.pallas import tpu as pltpu
from jax.sharding import PartitionSpec as P

O = 64
V = 512
BW = 8
F32 = jnp.float32
BF16 = jnp.bfloat16
MIB = 1 << 20
SMEM = pl.BlockSpec(memory_space=pltpu.SMEM)
VMEM = pl.BlockSpec(memory_space=pltpu.VMEM)
HBM = pl.BlockSpec(memory_space=pltpu.HBM)

SLOTS = ((1, 3), (5, 7), (2, 6), (4, 4))


def call(kernel, out_shape, n_scalars, n_arrays, scratch=(), flops=0, moved=0, limit=8):
    single = not isinstance(out_shape, tuple)
    return pl.pallas_call(
        kernel,
        out_shape=out_shape,
        in_specs=[SMEM] * n_scalars + [VMEM] * n_arrays,
        out_specs=VMEM if single else tuple(VMEM for _ in out_shape),
        scratch_shapes=list(scratch),
        compiler_params=pltpu.CompilerParams(vmem_limit_bytes=limit * MIB),
        cost_estimate=pl.CostEstimate(flops=flops, bytes_accessed=moved, transcendentals=0),
    )


def payload_kernel(occupied_ref, virtual_ref, out_ref, held, virtual, sems):
    chips = out_ref.shape[0]
    depth, cb = virtual_ref.shape
    first = pltpu.make_async_copy(virtual_ref, virtual, sems.at[0, chips])
    first.start()
    came = [
        pltpu.make_async_copy(occupied_ref.at[:, pl.ds(t * cb, cb)], held.at[t], sems.at[0, t])
        for t in range(chips)
    ]
    for copy in came:
        copy.start()
    first.wait()
    out = [
        pltpu.make_async_copy(virtual, out_ref.at[t, pl.ds(depth, depth)], sems.at[1, t])
        for t in range(chips)
    ]
    for copy in out:
        copy.start()
    for t in range(chips):
        came[t].wait()
        out.append(pltpu.make_async_copy(held.at[t], out_ref.at[t, pl.ds(0, depth)], sems.at[2, t]))
        out[-1].start()
    for copy in out:
        copy.wait()


def integrals_kernel(place_ref, factors_ref, kept_ref, sent_ref, total):
    sources, two_depth, cb = factors_ref.shape
    depth = two_depth // 2
    half = kept_ref.shape[0]
    occupied = factors_ref[:, :depth].reshape(sources * depth, cb)
    virtual = factors_ref[:, depth:].reshape(sources * depth, cb)
    total[...] = lax.dot_general(
        occupied, virtual, (((0,), (0,)), ((), ())), preferred_element_type=F32
    )
    core = place_ref[1]
    kept_ref[...] = total[pl.ds(pl.multiple_of(core * half, half), half), :]
    sent_ref[...] = total[pl.ds(pl.multiple_of((1 - core) * half, half), half), :]


def block_kernel(place_ref, kept_ref, came_ref, out_ref):
    kj, cb = kept_ref.shape
    ks = kj // O
    cs = cb // BW
    rows = O * BW
    integrals = (kept_ref[...] + came_ref[...]).astype(BF16)
    source = lax.broadcasted_iota(jnp.int32, (cb, cb), 0)
    target = lax.broadcasted_iota(jnp.int32, (cb, cb), 1)
    move = jnp.where(source == (target % cs) * BW + target // cs, 1.0, 0.0).astype(BF16)
    by_b = jnp.dot(integrals, move, preferred_element_type=F32).astype(BF16)
    stacked = jnp.concatenate(
        [
            jnp.concatenate(
                [by_b[k * O : (k + 1) * O, b * cs : (b + 1) * cs] for b in range(BW)], axis=0
            )
            for k in range(ks)
        ],
        axis=1,
    )
    row = lax.broadcasted_iota(jnp.int32, (rows, 1), 0)
    chunk = row // 256
    within = row % 128
    sender = place_ref[1] ^ ((row // 128) % 2)
    first = chunk == 0
    paired = first | (within < 64)
    slot = jnp.where(
        first,
        1 + 2 * sender + 4 * (within // 64),
        jnp.where(within < 64, 2 + 4 * sender, jnp.where(within < 96, 4, 0)),
    )
    core = jnp.where(paired, sender ^ ((within // 32) % 2), sender)
    j = (place_ref[0] ^ slot) * 8 + core * 4 + (within % 32) // BW
    wanted = (within % BW) * O + j
    source = lax.broadcasted_iota(jnp.int32, (rows, rows), 1)
    move = jnp.where(source == wanted, 1.0, 0.0).astype(BF16)
    out_ref[...] = jnp.dot(move, stacked, preferred_element_type=F32).astype(BF16)


def join(mine, refs, rows, staged, joined):
    width = refs[0].shape[1]
    ks = 4
    cs = width // ks
    for d, ref in enumerate(refs):
        staged[mine ^ d] = ref[rows, :]
    for k in range(ks):
        for pair in range(2):
            at = k * width + pair * 2 * cs
            joined[:, at : at + 2 * cs] = jnp.concatenate(
                [staged[2 * pair + i, :, k * cs : (k + 1) * cs] for i in range(2)], axis=1
            )


def columns_of(x, amplitudes_ref, into, tiles, sems):
    width = into.shape[1] // 4
    tile = into.shape[0] // tiles
    copies = []
    for m in range(tiles):
        for k in range(4):
            at = pl.multiple_of(k * 2 * width + x * width, width)
            rows = pl.ds(m * tile, tile)
            copies.append(
                pltpu.make_async_copy(
                    amplitudes_ref.at[rows, pl.ds(at, width)],
                    into.at[rows, pl.ds(k * width, width)],
                    sems.at[m, k],
                )
            )
    return copies


def far_columns_kernel(place_ref, amplitudes_ref, far_ref, sems):
    copies = columns_of(1 - place_ref[2], amplitudes_ref, far_ref, 2, sems)
    for copy in copies:
        copy.start()
    for copy in copies:
        copy.wait()


def near_kernel(tile, place_ref, b0, b1, b2, b3, amplitudes_ref, out_ref, held, staged, joined, sems):
    tiles = amplitudes_ref.shape[0] // tile
    copies = columns_of(place_ref[2], amplitudes_ref, held, tiles, sems)
    for copy in copies:
        copy.start()
    join(place_ref[3], (b0, b1, b2, b3), slice(None), staged, joined)
    for m in range(tiles):
        for copy in copies[4 * m : 4 * m + 4]:
            copy.wait()
        columns = slice(m * tile, (m + 1) * tile)
        out_ref[:, columns] = lax.dot_general(
            joined[...], held[columns, :], (((1,), (1,)), ((), ())), preferred_element_type=F32
        )


def far_kernel(tile, lo, place_ref, b0, b1, b2, b3, amplitudes_ref, near_ref, kept_ref, sent_ref, staged, joined):
    rows = joined.shape[0]
    half = rows // 2
    join(place_ref[3], (b0, b1, b2, b3), slice(lo, lo + rows), staged, joined)
    for m in range(amplitudes_ref.shape[0] // tile):
        columns = slice(m * tile, (m + 1) * tile)
        total = near_ref[lo : lo + rows, columns] + lax.dot_general(
            joined[...], amplitudes_ref[columns, :], (((1,), (1,)), ((), ())), preferred_element_type=F32
        )
        kept_ref[:, columns] = total[:half]
        sent_ref[:, columns] = total[half:].astype(BF16)


def per_device(amplitudes, occupied_factors, virtual_factors):
    kc_size = lax.axis_size("kc")
    ia_size = lax.axis_size("ia")
    chips = kc_size // 2
    kc = lax.axis_index("kc")
    ia = lax.axis_index("ia")
    place = jnp.stack([kc // 2, kc % 2, ia // 4, ia % 4]).astype(jnp.int32)
    same_core = [[2 * t + c for t in range(chips)] for c in range(2)]
    swap = [(i, i ^ 1) for i in range(kc_size)]
    depth, kj = occupied_factors.shape
    cb = virtual_factors.shape[1]
    local_rows, width = amplitudes.shape
    rows = O * BW
    share = rows // kc_size

    def over_ia(array, bits):
        return lax.ppermute(array, "ia", [(i, i ^ bits) for i in range(ia_size)])

    payload = pl.pallas_call(
        payload_kernel,
        out_shape=jax.ShapeDtypeStruct((chips, 2 * depth, cb), BF16),
        in_specs=[HBM, HBM],
        out_specs=HBM,
        scratch_shapes=[
            pltpu.VMEM((chips, depth, cb), BF16),
            pltpu.VMEM((depth, cb), BF16),
            pltpu.SemaphoreType.DMA((3, chips + 1)),
        ],
        compiler_params=pltpu.CompilerParams(vmem_limit_bytes=60 * MIB),
        cost_estimate=pl.CostEstimate(flops=0, bytes_accessed=4 * MIB, transcendentals=0),
    )(occupied_factors, virtual_factors)
    factors = lax.all_to_all(payload, "kc", 0, 0, axis_index_groups=same_core)
    held_far = pl.pallas_call(
        far_columns_kernel,
        out_shape=jax.ShapeDtypeStruct((local_rows, width // 2), BF16),
        in_specs=[SMEM, HBM],
        out_specs=VMEM,
        scratch_shapes=[pltpu.SemaphoreType.DMA((2, 4))],
        compiler_params=pltpu.CompilerParams(vmem_limit_bytes=40 * MIB),
        cost_estimate=pl.CostEstimate(flops=0, bytes_accessed=16 * MIB, transcendentals=0),
    )(place, amplitudes)
    factors, held_far = lax.optimization_barrier((factors, held_far))
    half = jax.ShapeDtypeStruct((kj // kc_size, cb), F32)
    kept, sent = call(
        integrals_kernel,
        (half, half),
        1,
        1,
        scratch=[pltpu.VMEM((kj // chips, cb), F32)],
        flops=2 * chips * depth * cb * cb,
        moved=3 * MIB,
    )(place, factors)
    came = lax.ppermute(sent, "kc", swap)
    own = call(
        block_kernel,
        jax.ShapeDtypeStruct((rows, width // ia_size), BF16),
        1,
        2,
        flops=4 * 512 * 512 * 256,
        moved=2 * MIB,
    )(place, kept, came)

    across = over_ia(own, 4)
    own1 = over_ia(own, 1)
    own3 = over_ia(own, 3)
    own2 = over_ia(own, 2)
    across1 = over_ia(across, 1)
    across3 = over_ia(across, 3)
    across2 = over_ia(own2, 4)

    tile = 1024
    flops = rows * local_rows * width
    near = pl.pallas_call(
        functools.partial(near_kernel, tile),
        out_shape=jax.ShapeDtypeStruct((rows, local_rows), F32),
        in_specs=[SMEM] + [VMEM] * 4 + [HBM],
        out_specs=VMEM,
        scratch_shapes=[
            pltpu.VMEM((local_rows, width // 2), BF16),
            pltpu.VMEM((4, rows, width // ia_size), BF16),
            pltpu.VMEM((rows, width // 2), BF16),
            pltpu.SemaphoreType.DMA((local_rows // tile, 4)),
        ],
        compiler_params=pltpu.CompilerParams(vmem_limit_bytes=36 * MIB),
        cost_estimate=pl.CostEstimate(flops=flops, bytes_accessed=17 * MIB, transcendentals=0),
    )(place, own, own1, own2, own3, amplitudes)

    def far(lo):
        part = rows // 4
        return call(
            functools.partial(far_kernel, tile, lo),
            (
                jax.ShapeDtypeStruct((part, local_rows), F32),
                jax.ShapeDtypeStruct((part, local_rows), BF16),
            ),
            1,
            6,
            scratch=[
                pltpu.VMEM((4, 2 * part, width // ia_size), BF16),
                pltpu.VMEM((2 * part, width // 2), BF16),
            ],
            flops=flops // 2,
            moved=12 * MIB,
        )(place, across, across1, across2, across3, held_far, near)

    def to_slot(array, bits):
        pairs = [(2 * t + c, 2 * (t ^ bits[c]) + c) for t in range(chips) for c in range(2)]
        return lax.ppermute(array, "kc", pairs)

    kept_a, sent_a = far(0)
    kept_b, sent_b = far(rows // 2)
    sums_a = kept_a + lax.ppermute(sent_a, "kc", swap).astype(F32)
    got0 = to_slot(sums_a[: 2 * share].astype(BF16), SLOTS[0])
    got1 = to_slot(sums_a[2 * share :].astype(BF16), SLOTS[1])
    sums_b = kept_b + lax.ppermute(sent_b, "kc", swap).astype(F32)
    got2 = to_slot(sums_b[: 2 * share].astype(BF16), SLOTS[2])
    got3 = to_slot(sums_b[2 * share : 3 * share].astype(BF16), SLOTS[3])
    got0, got1, got2, got3 = lax.optimization_barrier((got0, got1, got2, got3))
    got0, got1, got2, got3 = (got.astype(F32) for got in (got0, got1, got2, got3))
    mine = sums_b[3 * share :] + got0[:share] + got1[:share] + got2[:share] + got3
    other = got0[share:] + got1[share:] + got2[share:]
    return (mine + lax.ppermute(other, "kc", swap)).T


def solution(mesh):
    placed = (P("ia", "kc"), P("kc", None), P("kc", "ia"))
    return jax.shard_map(
        per_device, mesh=mesh, in_specs=placed, out_specs=P("ia", "kc"), check_vma=False
    )
```

time: 286 us -> 107 us (0.37)
  waiting for transfers between devices: 247 us -> 50.6 us
  starting transfers between devices: 0.09 us -> 27.8 us
  Pallas kernels: 0 us -> 22.8 us
  matrix products: 20.6 us -> 0 us
  between operations: 13.1 us -> 0.2 us
    reduce_scatter x2 -> x0, waiting for transfers between devices: 211 us -> none  [the longest x1 106 us: per_device(): return lax.psum_scatter(partial_sums, 'kc', scatter_dimension=1, tiled=True)]
    all_gather x1 -> x0, waiting for transfers between devices: 36.2 us -> none  [per_device(): lax.all_gather(blocks, 'ia', axis=1, tiled=True)]
    ppermute x0 -> x15, waiting for transfers between devices: none -> 31.9 us  [the longest x4 20.5 us: to_slot(): return lax.ppermute(array, 'kc', pairs)]
    pallas_call x0 -> x7, Pallas kernels: none -> 22.8 us  [the longest x1 7.45 us: per_device(): pl.pallas_call(functools.partial(near_kernel, tile), out_shape=jax.ShapeD...]
    dot_general x2 -> x0, matrix products: 20.6 us -> none  [the longest x1 15.2 us: per_device(): lax.dot_general(amplitude_view, lax.all_gather(blocks, 'ia', axis=1, tile...]
    ppermute x0 -> x15, starting transfers between devices: none -> 19.5 us  [the longest x4 8 us: to_slot(): return lax.ppermute(array, 'kc', pairs)]
    all_to_all x0 -> x1, waiting for transfers between devices: none -> 18.7 us  [per_device(): factors = lax.all_to_all(payload, 'kc', 0, 0, axis_index_groups=same_core)]
    all_to_all x0 -> x1, starting transfers between devices: none -> 8.34 us  [per_device(): factors = lax.all_to_all(payload, 'kc', 0, 0, axis_index_groups=same_core)]
  transfers between devices with their start and end apart: 3 -> 16, of which waited for: 3 -> 7; matrix products, arithmetic and copies ran while one was open for 0% -> 1% of each run, Pallas kernels for 0% -> 14%
where the time goes in v2:
time: 107 us
  waiting for transfers between devices  50.6 us (47%)
  starting transfers between devices  27.8 us (26%)
  Pallas kernels  22.8 us (21%)
  local copies, waits for them, and re-layouts  3.42 us (3%)
  other arithmetic  1.93 us (2%)
    ppermute x4, waiting for transfers between devices, to_slot(): return lax.ppermute(array, 'kc', pairs)  20.5 us
    all_to_all x1, waiting for transfers between devices, per_device(): factors = lax.all_to_all(payload, 'kc', 0, 0, axis_index_groups=same_core)  18.7 us
    all_to_all x1, starting transfers between devices, per_device(): factors = lax.all_to_all(payload, 'kc', 0, 0, axis_index_groups=same_core)  8.34 us
    ppermute x7, waiting for transfers between devices, over_ia(): return lax.ppermute(array, 'ia', [(i, i ^ bits) for i in range(ia_size)])  8.15 us
    ppermute x4, starting transfers between devices, to_slot(): return lax.ppermute(array, 'kc', pairs)  8 us
    ppermute x7, starting transfers between devices, over_ia(): return lax.ppermute(array, 'ia', [(i, i ^ bits) for i in range(ia_size)])  7.59 us
    pallas_call x1, Pallas kernels, per_device(): pl.pallas_call(functools.partial(near_kernel, tile), out_shape=jax.ShapeD...  7.45 us
    pallas_call x2, Pallas kernels, far(): call(functools.partial(far_kernel, tile, lo), (jax.ShapeDtypeStruct((part...  5.96 us
  transfers between devices with their start and end apart: 16, of which 7 were waited for; matrix products, arithmetic and copies ran while one was open for 1% of the time, Pallas kernels for 14%

profile of v2, /device:TPU:1, one launch (start us, length us, event | category | flops | bytes accessed | tf_op | source)
XLA Modules:
  0.0 106.8 jit_solution(12071824564586949966)
XLA Ops:
  0.0 2.5 %shard_map.37 = bf16[8,256,512]{2,1,0:T(8,128)(2,1)} custom-call(bf16[128,4096]{1,0:T(8,128)(2,1)} %occupied_ref.1, bf16[128,512]{1,0:T(8,128)(2,1)} %virtual_ref.1), custom_call_target="tpu_custom_call" | custom-call | bytes 4194304 | tf_op jit(solution)/shard_map/pallas_call | solution.py:200
  2.5 8.3 %all-to-all-start = ((bf16[8,256,512]{2,1,0:T(8,128)(2,1)}), bf16[8,256,512]{2,1,0:T(8,128)(2,1)S(1)}, u32[]{:S(2)}, u32[]{:S(2)}) async-start(bf16[8,256,512]{2,1,0:T(8,128)(2,1)} %shard_map.37), calls=%async_computation | async-start | bytes 4194304 | tf_op jit(solution)/shard_map/all_to_all | solution.py:213
  10.9 0.1 pad_add_fusion.place_ref
  11.0 4.1 %shard_map.38.amplitudes_ref = bf16[4096,1024]{1,0:T(8,128)(2,1)S(1)} custom-call(s32[4]{0:T(128)S(1)} %pad_add_fusion.place_ref, bf16[4096,2048]{1,0:T(8,128)(2,1)} %amplitudes_ref.3), custom_call_target="tpu_custom_call" | custom-call | bytes 16777216 | tf_op jit(solution)/shard_map/pallas_call | solution.py:214
  15.1 3.3 %copy-done = bf16[4096,1024]{1,0:T(8,128)(2,1)} copy-done((bf16[4096,1024]{1,0:T(8,128)(2,1)}, bf16[4096,1024]{1,0:T(8,128)(2,1)S(1)}, u32[]{:S(2)}) %copy-start) | copy-done | bytes 8388632
  18.4 18.7 %all-to-all-done.factors_ref = bf16[8,256,512]{2,1,0:T(8,128)(2,1)S(1)} async-done(((bf16[8,256,512]{2,1,0:T(8,128)(2,1)}), bf16[8,256,512]{2,1,0:T(8,128)(2,1)S(1)}, u32[]{:S(2)}, u32[]{:S(2)}) %all-to-all-start) | async-done | bytes 2097184 | tf_op jit(solution)/shard_map/all_to_all | solution.py:213
  37.0 1.3 %shard_map.39 = (f32[256,512]{1,0:T(8,128)S(1)}, f32[256,512]{1,0:T(8,128)S(1)}) custom-call(s32[4]{0:T(128)S(1)} %pad_add_fusion.place_ref, bf16[8,256,512]{2,1,0:T(8,128)(2,1)S(1)} %all-to-all-done.factors_ref), custom_call_target="tpu_custom_call" | custom-call | flops 536870912 | bytes 3145728 | tf_op jit(solution)/shard_map/pallas_call | solution.py:225
  38.4 1.3 %collective-permute-start = (f32[256,512]{1,0:T(8,128)S(1)}, f32[256,512]{1,0:T(8,128)S(1)}, u32[]{:S(2)}, u32[]{:S(2)}) collective-permute-start(f32[256,512]{1,0:T(8,128)S(1)} %get-tuple-element.19), channel_id=1, source_target_pairs={{0,8},{8,0},{16,24},{24,16},{32,40},{40,32},{48,56},{56,48},{64,72... | collective-permute-start | bytes 1572872 | tf_op jit(solution)/shard_map/ppermute | solution.py:234
  39.7 1.5 %collective-permute-done.came_ref = f32[256,512]{1,0:T(8,128)S(1)} collective-permute-done((f32[256,512]{1,0:T(8,128)S(1)}, f32[256,512]{1,0:T(8,128)S(1)}, u32[]{:S(2)}, u32[]{:S(2)}) %collective-permute-start) | collective-permute-done | bytes 524320 | tf_op jit(solution)/shard_map/ppermute | solution.py:234
  41.2 1.4 %shard_map.40.b0 = bf16[512,256]{1,0:T(8,128)(2,1)S(1)} custom-call(s32[4]{0:T(128)S(1)} %pad_add_fusion.place_ref, f32[256,512]{1,0:T(8,128)S(1)} %get-tuple-element.18.kept_ref, f32[256,512]{1,0:T(8,128)S(1)} %collective-permute-done.came_ref), custom_call_target="tpu_custom_call" | custom-call | flops 268435456 | bytes 2097152 | tf_op jit(solution)/shard_map/pallas_call | solution.py:235
  42.6 0.0 slice-start.1
  42.6 0.4 collective-permute-start.1
  43.0 2.9 %collective-permute-start.3 = (bf16[512,256]{1,0:T(8,128)(2,1)S(1)}, bf16[512,256]{1,0:T(8,128)(2,1)S(1)}, u32[]{:S(2)}, u32[]{:S(2)}) collective-permute-start(bf16[512,256]{1,0:T(8,128)(2,1)S(1)} %shard_map.40.b0), channel_id=1, source_target_pairs={{0,2},{1,3},{2,0},{3,1},{4,6},{5,7},{6,4},{7,5},{8,10},{9,11},{10,... | collective-permute-start | bytes 786440 | tf_op jit(solution)/shard_map/ppermute | solution.py:198
  45.9 0.4 collective-permute-start.6
  46.3 0.4 collective-permute-start.7
  46.7 3.5 %collective-permute-done.1.b0 = bf16[512,256]{1,0:T(8,128)(2,1)S(1)} collective-permute-done((bf16[512,256]{1,0:T(8,128)(2,1)S(1)}, bf16[512,256]{1,0:T(8,128)(2,1)S(1)}, u32[]{:S(2)}, u32[]{:S(2)}) %collective-permute-start.1) | collective-permute-done | bytes 262176 | tf_op jit(solution)/shard_map/ppermute | solution.py:198
  50.2 1.3 %collective-permute-start.2 = (bf16[512,256]{1,0:T(8,128)(2,1)S(1)}, bf16[512,256]{1,0:T(8,128)(2,1)S(1)}, u32[]{:S(2)}, u32[]{:S(2)}) collective-permute-start(bf16[512,256]{1,0:T(8,128)(2,1)S(1)} %collective-permute-done.1.b0), channel_id=1, source_target_pairs={{0,1},{1,0},{2,3},{3,2},{4,5},{5,4},{6,7},{7,6},{8,9},{9,8},{10,11... | collective-permute-start | bytes 786440 | tf_op jit(solution)/shard_map/ppermute | solution.py:198
  51.5 1.9 %collective-permute-start.5 = (bf16[512,256]{1,0:T(8,128)(2,1)S(1)}, bf16[512,256]{1,0:T(8,128)(2,1)S(1)}, u32[]{:S(2)}, u32[]{:S(2)}) collective-permute-start(bf16[512,256]{1,0:T(8,128)(2,1)S(1)} %collective-permute-done.1.b0), channel_id=1, source_target_pairs={{0,3},{1,2},{2,1},{3,0},{4,7},{5,6},{6,5},{7,4},{8,11},{9,10},{10,... | collective-permute-start | bytes 786440 | tf_op jit(solution)/shard_map/ppermute | solution.py:198
  53.4 0.0 collective-permute-done.3.b2
  53.4 0.3 collective-permute-start.4
  53.7 4.0 %collective-permute-done.6.b1 = bf16[512,256]{1,0:T(8,128)(2,1)S(1)} collective-permute-done((bf16[512,256]{1,0:T(8,128)(2,1)S(1)}, bf16[512,256]{1,0:T(8,128)(2,1)S(1)}, u32[]{:S(2)}, u32[]{:S(2)}) %collective-permute-start.6) | collective-permute-done | bytes 262176 | tf_op jit(solution)/shard_map/ppermute | solution.py:198
  57.7 0.6 collective-permute-done.7.b3
  58.3 7.4 %shard_map.41.near_ref = f32[512,4096]{1,0:T(8,128)S(1)} custom-call(s32[4]{0:T(128)S(1)} %pad_add_fusion.place_ref, bf16[512,256]{1,0:T(8,128)(2,1)S(1)} %shard_map.40.b0, bf16[512,256]{1,0:T(8,128)(2,1)S(1)} %collective-permute-done.6.b1, bf16[512,256]{1,0:T(8,128)(2,1)S(1)} %collective-permute-done.3.b2, bf16[512,256]{1,0:T(8,128)(2,1)S(1)} %collective-permute-done.7.b3, ...), custom_call_target="tpu_custom_call" | custom-call | flops 4294967296 | bytes 17825792 | tf_op jit(solution)/shard_map/pallas_call | solution.py:254
  65.8 0.0 collective-permute-done.2.b1
  65.8 0.0 collective-permute-done.4.b2
  65.8 3.0 %shard_map.43 = (f32[128,4096]{1,0:T(8,128)S(1)}, bf16[128,4096]{1,0:T(8,128)(2,1)S(1)}) custom-call(s32[4]{0:T(128)S(1)} %pad_add_fusion.place_ref, bf16[512,256]{1,0:T(8,128)(2,1)S(1)} %collective-permute-done.1.b0, bf16[512,256]{1,0:T(8,128)(2,1)S(1)} %collective-permute-done.2.b1, bf16[512,256]{1,0:T(8,128)(2,1)S(1)} %collective-permute-done.4.b2, ...), custom_call_target="tpu_custom_call" | custom-call | flops 2147483648 | bytes 12582912 | tf_op jit(solution)/shard_map/pallas_call | solution.py:271
  68.8 2.3 %collective-permute-start.9 = (bf16[128,4096]{1,0:T(8,128)(2,1)S(1)}, bf16[128,4096]{1,0:T(8,128)(2,1)S(1)}, u32[]{:S(2)}, u32[]{:S(2)}) collective-permute-start(bf16[128,4096]{1,0:T(8,128)(2,1)S(1)} %get-tuple-element.24), channel_id=1, source_target_pairs={{0,8},{8,0},{16,24},{24,16},{32,40},{40,32},{48,56},{56,48},{64,72... | collective-permute-start | bytes 3145736 | tf_op jit(solution)/shard_map/ppermute | solution.py:293
  71.1 3.0 %shard_map.42 = (f32[128,4096]{1,0:T(8,128)S(1)}, bf16[128,4096]{1,0:T(8,128)(2,1)S(1)}) custom-call(s32[4]{0:T(128)S(1)} %pad_add_fusion.place_ref, bf16[512,256]{1,0:T(8,128)(2,1)S(1)} %collective-permute-done.1.b0, bf16[512,256]{1,0:T(8,128)(2,1)S(1)} %collective-permute-done.2.b1, bf16[512,256]{1,0:T(8,128)(2,1)S(1)} %collective-permute-done.4.b2, ...), custom_call_target="tpu_custom_call" | custom-call | flops 2147483648 | bytes 12582912 | tf_op jit(solution)/shard_map/pallas_call | solution.py:271
  74.1 0.1 collective-permute-start.8
  74.2 0.0 collective-permute-done.9
  74.2 0.3 add_convert_fusion
  74.5 0.1 fusion.4
  74.6 2.8 %collective-permute-start.10 = (bf16[64,4096]{1,0:T(8,128)(2,1)S(1)}, bf16[64,4096]{1,0:T(8,128)(2,1)S(1)}, u32[]{:S(2)}, u32[]{:S(2)}) collective-permute-start(bf16[64,4096]{1,0:T(8,128)(2,1)S(1)} %get-tuple-element.32), channel_id=1, source_target_pairs={{0,16},{8,56},{16,0},{24,40},{32,48},{40,24},{48,32},{56,8},{64,80... | collective-permute-start | bytes 1572872 | tf_op jit(solution)/shard_map/ppermute | solution.py:289
  77.4 2.6 %collective-permute-start.11 = (bf16[64,4096]{1,0:T(8,128)(2,1)S(1)}, bf16[64,4096]{1,0:T(8,128)(2,1)S(1)}, u32[]{:S(2)}, u32[]{:S(2)}) collective-permute-start(bf16[64,4096]{1,0:T(8,128)(2,1)S(1)} %get-tuple-element.31), channel_id=1, source_target_pairs={{0,80},{8,120},{16,64},{24,104},{32,112},{40,88},{48,96},{56,72},{... | collective-permute-start | bytes 1572872 | tf_op jit(solution)/shard_map/ppermute | solution.py:289
  79.9 0.0 collective-permute-done.8
  79.9 0.3 fusion.3
  80.3 1.3 %collective-permute-start.12 = (bf16[64,4096]{1,0:T(8,128)(2,1)S(1)}, bf16[64,4096]{1,0:T(8,128)(2,1)S(1)}, u32[]{:S(2)}, u32[]{:S(2)}) collective-permute-start(bf16[64,4096]{1,0:T(8,128)(2,1)S(1)} %slice.51), channel_id=1, source_target_pairs={{0,32},{8,104},{16,48},{24,120},{32,0},{40,72},{48,16},{56,88},{64... | collective-permute-start | bytes 1572872 | tf_op jit(solution)/shard_map/ppermute | solution.py:289
  81.7 1.3 %collective-permute-start.13 = (bf16[32,4096]{1,0:T(8,128)(2,1)S(1)}, bf16[32,4096]{1,0:T(8,128)(2,1)S(1)}, u32[]{:S(2)}, u32[]{:S(2)}) collective-permute-start(bf16[32,4096]{1,0:T(8,128)(2,1)S(1)} %slice.52), channel_id=1, source_target_pairs={{0,64},{8,72},{16,80},{24,88},{32,96},{40,104},{48,112},{56,120},{... | collective-permute-start | bytes 786440 | tf_op jit(solution)/shard_map/ppermute | solution.py:289
  83.0 20.5 %collective-permute-done.13 = bf16[32,4096]{1,0:T(8,128)(2,1)S(1)} collective-permute-done((bf16[32,4096]{1,0:T(8,128)(2,1)S(1)}, bf16[32,4096]{1,0:T(8,128)(2,1)S(1)}, u32[]{:S(2)}, u32[]{:S(2)}) %collective-permute-start.13) | collective-permute-done | bytes 262176 | tf_op jit(solution)/shard_map/ppermute | solution.py:289
  103.4 0.0 collective-permute-done.10
  103.4 0.0 collective-permute-done.11
  103.5 0.1 convert_element_type.26
  103.5 0.1 convert_element_type.25
  103.6 0.1 convert_element_type.24
  103.7 0.1 slice_add_fusion
  103.8 0.2 collective-permute-start.14
  104.0 1.7 %collective-permute-done.14 = f32[32,4096]{1,0:T(8,128)S(1)} collective-permute-done((f32[32,4096]{1,0:T(8,128)S(1)}, f32[32,4096]{1,0:T(8,128)S(1)}, u32[]{:S(2)}, u32[]{:S(2)}) %collective-permute-start.14) | collective-permute-done | bytes 524320 | tf_op jit(solution)/shard_map/ppermute | solution.py:303
  105.8 1.0 fusion.2
  (9 shorter events, 0.1 us)
Async XLA Ops:
  2.5 34.5 %all-to-all-start = ((bf16[8,256,512]{2,1,0:T(8,128)(2,1)}), bf16[8,256,512]{2,1,0:T(8,128)(2,1)S(1)}, u32[]{:S(2)}, u32[]{:S(2)}) async-start(bf16[8,256,512]{2,1,0:T(8,128)(2,1)} %shard_map.37), calls=%async_computation | async-start | bytes 4194304 | tf_op jit(solution)/shard_map/all_to_all | solution.py:213
  15.1 3.3 %copy-start = (bf16[4096,1024]{1,0:T(8,128)(2,1)}, bf16[4096,1024]{1,0:T(8,128)(2,1)S(1)}, u32[]{:S(2)}) copy-start(bf16[4096,1024]{1,0:T(8,128)(2,1)S(1)} %shard_map.38.amplitudes_ref) | copy-start | bytes 25165828
  38.4 2.8 %collective-permute-start = (f32[256,512]{1,0:T(8,128)S(1)}, f32[256,512]{1,0:T(8,128)S(1)}, u32[]{:S(2)}, u32[]{:S(2)}) collective-permute-start(f32[256,512]{1,0:T(8,128)S(1)} %get-tuple-element.19), channel_id=1, source_target_pairs={{0,8},{8,0},{16,24},{24,16},{32,40},{40,32},{48,56},{56,48},{64,72... | collective-permute-start | bytes 1572872 | tf_op jit(solution)/shard_map/ppermute | solution.py:234
  41.2 24.6 %slice-start = ((s8[8388608]{0:T(1024)(128)(4,1)}), s8[4194304]{0:T(1024)(128)(4,1)S(1)}, s32[]{:S(2)}) async-start(s8[8388608]{0:T(1024)(128)(4,1)} %bitcast.6), calls=%async_computation.1 | async-start | bytes 8388608
  42.6 23.2 %slice-start.1 = ((s8[8388608]{0:T(1024)(128)(4,1)}), s8[4194304]{0:T(1024)(128)(4,1)S(1)}, s32[]{:S(2)}) async-start(s8[8388608]{0:T(1024)(128)(4,1)} %bitcast.6), calls=%async_computation.2 | async-start | bytes 8388608
  42.6 7.6 %collective-permute-start.1 = (bf16[512,256]{1,0:T(8,128)(2,1)S(1)}, bf16[512,256]{1,0:T(8,128)(2,1)S(1)}, u32[]{:S(2)}, u32[]{:S(2)}) collective-permute-start(bf16[512,256]{1,0:T(8,128)(2,1)S(1)} %shard_map.40.b0), channel_id=1, source_target_pairs={{0,4},{1,5},{2,6},{3,7},{4,0},{5,1},{6,2},{7,3},{8,12},{9,13},{10,... | collective-permute-start | bytes 786440 | tf_op jit(solution)/shard_map/ppermute | solution.py:198
  43.0 10.4 %collective-permute-start.3 = (bf16[512,256]{1,0:T(8,128)(2,1)S(1)}, bf16[512,256]{1,0:T(8,128)(2,1)S(1)}, u32[]{:S(2)}, u32[]{:S(2)}) collective-permute-start(bf16[512,256]{1,0:T(8,128)(2,1)S(1)} %shard_map.40.b0), channel_id=1, source_target_pairs={{0,2},{1,3},{2,0},{3,1},{4,6},{5,7},{6,4},{7,5},{8,10},{9,11},{10,... | collective-permute-start | bytes 786440 | tf_op jit(solution)/shard_map/ppermute | solution.py:198
  45.9 11.8 %collective-permute-start.6 = (bf16[512,256]{1,0:T(8,128)(2,1)S(1)}, bf16[512,256]{1,0:T(8,128)(2,1)S(1)}, u32[]{:S(2)}, u32[]{:S(2)}) collective-permute-start(bf16[512,256]{1,0:T(8,128)(2,1)S(1)} %shard_map.40.b0), channel_id=1, source_target_pairs={{0,1},{1,0},{2,3},{3,2},{4,5},{5,4},{6,7},{7,6},{8,9},{9,8},{10,11... | collective-permute-start | bytes 786440 | tf_op jit(solution)/shard_map/ppermute | solution.py:198
  46.3 12.0 %collective-permute-start.7 = (bf16[512,256]{1,0:T(8,128)(2,1)S(1)}, bf16[512,256]{1,0:T(8,128)(2,1)S(1)}, u32[]{:S(2)}, u32[]{:S(2)}) collective-permute-start(bf16[512,256]{1,0:T(8,128)(2,1)S(1)} %shard_map.40.b0), channel_id=1, source_target_pairs={{0,3},{1,2},{2,1},{3,0},{4,7},{5,6},{6,5},{7,4},{8,11},{9,10},{10,... | collective-permute-start | bytes 786440 | tf_op jit(solution)/shard_map/ppermute | solution.py:198
  50.2 15.6 %collective-permute-start.2 = (bf16[512,256]{1,0:T(8,128)(2,1)S(1)}, bf16[512,256]{1,0:T(8,128)(2,1)S(1)}, u32[]{:S(2)}, u32[]{:S(2)}) collective-permute-start(bf16[512,256]{1,0:T(8,128)(2,1)S(1)} %collective-permute-done.1.b0), channel_id=1, source_target_pairs={{0,1},{1,0},{2,3},{3,2},{4,5},{5,4},{6,7},{7,6},{8,9},{9,8},{10,11... | collective-permute-start | bytes 786440 | tf_op jit(solution)/shard_map/ppermute | solution.py:198
  51.5 14.3 %collective-permute-start.5 = (bf16[512,256]{1,0:T(8,128)(2,1)S(1)}, bf16[512,256]{1,0:T(8,128)(2,1)S(1)}, u32[]{:S(2)}, u32[]{:S(2)}) collective-permute-start(bf16[512,256]{1,0:T(8,128)(2,1)S(1)} %collective-permute-done.1.b0), channel_id=1, source_target_pairs={{0,3},{1,2},{2,1},{3,0},{4,7},{5,6},{6,5},{7,4},{8,11},{9,10},{10,... | collective-permute-start | bytes 786440 | tf_op jit(solution)/shard_map/ppermute | solution.py:198
  53.4 12.4 %collective-permute-start.4 = (bf16[512,256]{1,0:T(8,128)(2,1)S(1)}, bf16[512,256]{1,0:T(8,128)(2,1)S(1)}, u32[]{:S(2)}, u32[]{:S(2)}) collective-permute-start(bf16[512,256]{1,0:T(8,128)(2,1)S(1)} %collective-permute-done.3.b2), channel_id=1, source_target_pairs={{0,4},{1,5},{2,6},{3,7},{4,0},{5,1},{6,2},{7,3},{8,12},{9,13},{10,... | collective-permute-start | bytes 786440 | tf_op jit(solution)/shard_map/ppermute | solution.py:198
  68.8 5.4 %collective-permute-start.9 = (bf16[128,4096]{1,0:T(8,128)(2,1)S(1)}, bf16[128,4096]{1,0:T(8,128)(2,1)S(1)}, u32[]{:S(2)}, u32[]{:S(2)}) collective-permute-start(bf16[128,4096]{1,0:T(8,128)(2,1)S(1)} %get-tuple-element.24), channel_id=1, source_target_pairs={{0,8},{8,0},{16,24},{24,16},{32,40},{40,32},{48,56},{56,48},{64,72... | collective-permute-start | bytes 3145736 | tf_op jit(solution)/shard_map/ppermute | solution.py:293
  74.1 5.9 %collective-permute-start.8 = (bf16[128,4096]{1,0:T(8,128)(2,1)S(1)}, bf16[128,4096]{1,0:T(8,128)(2,1)S(1)}, u32[]{:S(2)}, u32[]{:S(2)}) collective-permute-start(bf16[128,4096]{1,0:T(8,128)(2,1)S(1)} %get-tuple-element.22), channel_id=1, source_target_pairs={{0,8},{8,0},{16,24},{24,16},{32,40},{40,32},{48,56},{56,48},{64,72... | collective-permute-start | bytes 3145736 | tf_op jit(solution)/shard_map/ppermute | solution.py:296
  74.6 28.9 %collective-permute-start.10 = (bf16[64,4096]{1,0:T(8,128)(2,1)S(1)}, bf16[64,4096]{1,0:T(8,128)(2,1)S(1)}, u32[]{:S(2)}, u32[]{:S(2)}) collective-permute-start(bf16[64,4096]{1,0:T(8,128)(2,1)S(1)} %get-tuple-element.32), channel_id=1, source_target_pairs={{0,16},{8,56},{16,0},{24,40},{32,48},{40,24},{48,32},{56,8},{64,80... | collective-permute-start | bytes 1572872 | tf_op jit(solution)/shard_map/ppermute | solution.py:289
  77.4 26.1 %collective-permute-start.11 = (bf16[64,4096]{1,0:T(8,128)(2,1)S(1)}, bf16[64,4096]{1,0:T(8,128)(2,1)S(1)}, u32[]{:S(2)}, u32[]{:S(2)}) collective-permute-start(bf16[64,4096]{1,0:T(8,128)(2,1)S(1)} %get-tuple-element.31), channel_id=1, source_target_pairs={{0,80},{8,120},{16,64},{24,104},{32,112},{40,88},{48,96},{56,72},{... | collective-permute-start | bytes 1572872 | tf_op jit(solution)/shard_map/ppermute | solution.py:289
  80.3 23.1 %collective-permute-start.12 = (bf16[64,4096]{1,0:T(8,128)(2,1)S(1)}, bf16[64,4096]{1,0:T(8,128)(2,1)S(1)}, u32[]{:S(2)}, u32[]{:S(2)}) collective-permute-start(bf16[64,4096]{1,0:T(8,128)(2,1)S(1)} %slice.51), channel_id=1, source_target_pairs={{0,32},{8,104},{16,48},{24,120},{32,0},{40,72},{48,16},{56,88},{64... | collective-permute-start | bytes 1572872 | tf_op jit(solution)/shard_map/ppermute | solution.py:289
  81.7 21.8 %collective-permute-start.13 = (bf16[32,4096]{1,0:T(8,128)(2,1)S(1)}, bf16[32,4096]{1,0:T(8,128)(2,1)S(1)}, u32[]{:S(2)}, u32[]{:S(2)}) collective-permute-start(bf16[32,4096]{1,0:T(8,128)(2,1)S(1)} %slice.52), channel_id=1, source_target_pairs={{0,64},{8,72},{16,80},{24,88},{32,96},{40,104},{48,112},{56,120},{... | collective-permute-start | bytes 786440 | tf_op jit(solution)/shard_map/ppermute | solution.py:289
  103.8 2.0 %collective-permute-start.14 = (f32[32,4096]{1,0:T(8,128)S(1)}, f32[32,4096]{1,0:T(8,128)S(1)}, u32[]{:S(2)}, u32[]{:S(2)}) collective-permute-start(f32[32,4096]{1,0:T(8,128)S(1)} %slice_add_fusion), channel_id=1, source_target_pairs={{0,8},{8,0},{16,24},{24,16},{32,40},{40,32},{48,56},{56,48},{64,72... | collective-permute-start | bytes 1572872 | tf_op jit(solution)/shard_map/ppermute | solution.py:303

commit v3 on v2

--- a/solution.py
+++ b/solution.py
@@ -17,7 +17,7 @@
 VMEM = pl.BlockSpec(memory_space=pltpu.VMEM)
 HBM = pl.BlockSpec(memory_space=pltpu.HBM)
 
-SLOTS = ((1, 3), (5, 7), (2, 6), (4, 4))
+SLOTS = ((5, 7), (2, 6), (1, 3), (4, 4))
 
 
 def call(kernel, out_shape, n_scalars, n_arrays, scratch=(), flops=0, moved=0, limit=8):
@@ -100,8 +100,8 @@
     paired = first | (within < 64)
     slot = jnp.where(
         first,
-        1 + 2 * sender + 4 * (within // 64),
-        jnp.where(within < 64, 2 + 4 * sender, jnp.where(within < 96, 4, 0)),
+        jnp.where(within < 64, 5 + 2 * sender, 2 + 4 * sender),
+        jnp.where(within < 64, 1 + 2 * sender, jnp.where(within < 96, 4, 0)),
     )
     core = jnp.where(paired, sender ^ ((within // 32) % 2), sender)
     j = (place_ref[0] ^ slot) * 8 + core * 4 + (within % 32) // BW
@@ -143,26 +143,20 @@
     return copies
 
 
-def far_columns_kernel(place_ref, amplitudes_ref, far_ref, sems):
-    copies = columns_of(1 - place_ref[2], amplitudes_ref, far_ref, 2, sems)
+def columns_kernel(far, place_ref, amplitudes_ref, out_ref, sems):
+    copies = columns_of(place_ref[2] ^ far, amplitudes_ref, out_ref, 2, sems)
     for copy in copies:
         copy.start()
     for copy in copies:
         copy.wait()
 
 
-def near_kernel(tile, place_ref, b0, b1, b2, b3, amplitudes_ref, out_ref, held, staged, joined, sems):
-    tiles = amplitudes_ref.shape[0] // tile
-    copies = columns_of(place_ref[2], amplitudes_ref, held, tiles, sems)
-    for copy in copies:
-        copy.start()
+def near_kernel(tile, place_ref, b0, b1, b2, b3, held_ref, out_ref, staged, joined):
     join(place_ref[3], (b0, b1, b2, b3), slice(None), staged, joined)
-    for m in range(tiles):
-        for copy in copies[4 * m : 4 * m + 4]:
-            copy.wait()
+    for m in range(held_ref.shape[0] // tile):
         columns = slice(m * tile, (m + 1) * tile)
         out_ref[:, columns] = lax.dot_general(
-            joined[...], held[columns, :], (((1,), (1,)), ((), ())), preferred_element_type=F32
+            joined[...], held_ref[columns, :], (((1,), (1,)), ((), ())), preferred_element_type=F32
         )
 
 
@@ -211,15 +205,18 @@
         cost_estimate=pl.CostEstimate(flops=0, bytes_accessed=4 * MIB, transcendentals=0),
     )(occupied_factors, virtual_factors)
     factors = lax.all_to_all(payload, "kc", 0, 0, axis_index_groups=same_core)
-    held_far = pl.pallas_call(
-        far_columns_kernel,
-        out_shape=jax.ShapeDtypeStruct((local_rows, width // 2), BF16),
-        in_specs=[SMEM, HBM],
-        out_specs=VMEM,
-        scratch_shapes=[pltpu.SemaphoreType.DMA((2, 4))],
-        compiler_params=pltpu.CompilerParams(vmem_limit_bytes=40 * MIB),
-        cost_estimate=pl.CostEstimate(flops=0, bytes_accessed=16 * MIB, transcendentals=0),
-    )(place, amplitudes)
+    def columns(far, where):
+        return pl.pallas_call(
+            functools.partial(columns_kernel, far),
+            out_shape=jax.ShapeDtypeStruct((local_rows, width // 2), BF16),
+            in_specs=[SMEM, HBM],
+            out_specs=VMEM,
+            scratch_shapes=[pltpu.SemaphoreType.DMA((2, 4))],
+            compiler_params=pltpu.CompilerParams(vmem_limit_bytes=36 * MIB),
+            cost_estimate=pl.CostEstimate(flops=0, bytes_accessed=16 * MIB, transcendentals=0),
+        )(where, amplitudes)
+
+    held_far = columns(1, place)
     factors, held_far = lax.optimization_barrier((factors, held_far))
     half = jax.ShapeDtypeStruct((kj // kc_size, cb), F32)
     kept, sent = call(
@@ -241,6 +238,7 @@
         moved=2 * MIB,
     )(place, kept, came)
 
+    near_place, _ = lax.optimization_barrier((place, own))
     across = over_ia(own, 4)
     own1 = over_ia(own, 1)
     own3 = over_ia(own, 3)
@@ -251,20 +249,16 @@
 
     tile = 1024
     flops = rows * local_rows * width
-    near = pl.pallas_call(
+    held_near = columns(0, near_place)
+    near = call(
         functools.partial(near_kernel, tile),
-        out_shape=jax.ShapeDtypeStruct((rows, local_rows), F32),
-        in_specs=[SMEM] + [VMEM] * 4 + [HBM],
-        out_specs=VMEM,
-        scratch_shapes=[
-            pltpu.VMEM((local_rows, width // 2), BF16),
-            pltpu.VMEM((4, rows, width // ia_size), BF16),
-            pltpu.VMEM((rows, width // 2), BF16),
-            pltpu.SemaphoreType.DMA((local_rows // tile, 4)),
-        ],
-        compiler_params=pltpu.CompilerParams(vmem_limit_bytes=36 * MIB),
-        cost_estimate=pl.CostEstimate(flops=flops, bytes_accessed=17 * MIB, transcendentals=0),
-    )(place, own, own1, own2, own3, amplitudes)
+        jax.ShapeDtypeStruct((rows, local_rows), F32),
+        1,
+        5,
+        scratch=[pltpu.VMEM((4, rows, width // ia_size), BF16), pltpu.VMEM((rows, width // 2), BF16)],
+        flops=flops,
+        moved=17 * MIB,
+    )(place, own, own1, own2, own3, held_near)
 
     def far(lo):
         part = rows // 4
@@ -296,11 +290,11 @@
     sums_b = kept_b + lax.ppermute(sent_b, "kc", swap).astype(F32)
     got2 = to_slot(sums_b[: 2 * share].astype(BF16), SLOTS[2])
     got3 = to_slot(sums_b[2 * share : 3 * share].astype(BF16), SLOTS[3])
-    got0, got1, got2, got3 = lax.optimization_barrier((got0, got1, got2, got3))
-    got0, got1, got2, got3 = (got.astype(F32) for got in (got0, got1, got2, got3))
-    mine = sums_b[3 * share :] + got0[:share] + got1[:share] + got2[:share] + got3
-    other = got0[share:] + got1[share:] + got2[share:]
-    return (mine + lax.ppermute(other, "kc", swap)).T
+    mine = sums_b[3 * share :] + got0[:share].astype(F32) + got1[:share].astype(F32) + got3.astype(F32)
+    other = got0[share:].astype(F32) + got1[share:].astype(F32)
+    mine, other, got2 = lax.optimization_barrier((mine, other, got2))
+    other = other + got2[share:].astype(F32)
+    return (mine + got2[:share].astype(F32) + lax.ppermute(other, "kc", swap)).T
 
 
 def solution(mesh):

time: 107 us -> 104 us (0.972)
  waiting for transfers between devices: 50.6 us -> 46.1 us
  Pallas kernels: 22.8 us -> 24.6 us
    ppermute x7, waiting for transfers between devices: 8.15 us -> 3.93 us  [over_ia(): return lax.ppermute(array, 'ia', [(i, i ^ bits) for i in range(ia_size)])]
    pallas_call x2 -> x3, Pallas kernels: 11.6 us -> 13.4 us  [the longest x2 8.26 us: columns(): pl.pallas_call(functools.partial(columns_kernel, far), out_shape=jax.Shap...]
  transfers between devices with their start and end apart: 16 -> 16, of which waited for: 7 -> 8; matrix products, arithmetic and copies ran while one was open for 1% -> 1% of each run, Pallas kernels for 14% -> 16%
where the time goes in v3:
time: 104 us
  waiting for transfers between devices  46.1 us (44%)
  starting transfers between devices  28.1 us (27%)
  Pallas kernels  24.6 us (24%)
  local copies, waits for them, and re-layouts  3.42 us (3%)
  other arithmetic  1.66 us (2%)
    ppermute x4, waiting for transfers between devices, to_slot(): return lax.ppermute(array, 'kc', pairs)  20.3 us
    all_to_all x1, waiting for transfers between devices, per_device(): factors = lax.all_to_all(payload, 'kc', 0, 0, axis_index_groups=same_core)  18.7 us
    all_to_all x1, starting transfers between devices, per_device(): factors = lax.all_to_all(payload, 'kc', 0, 0, axis_index_groups=same_core)  8.34 us
    ppermute x4, starting transfers between devices, to_slot(): return lax.ppermute(array, 'kc', pairs)  8.28 us
    pallas_call x2, Pallas kernels, columns(): pl.pallas_call(functools.partial(columns_kernel, far), out_shape=jax.Shap...  8.26 us
    ppermute x7, starting transfers between devices, over_ia(): return lax.ppermute(array, 'ia', [(i, i ^ bits) for i in range(ia_size)])  8.08 us
    pallas_call x2, Pallas kernels, far(): call(functools.partial(far_kernel, tile, lo), (jax.ShapeDtypeStruct((part...  5.95 us
    pallas_call x1, Pallas kernels, per_device(): call(functools.partial(near_kernel, tile), jax.ShapeDtypeStruct((rows, lo...  5.17 us
  transfers between devices with their start and end apart: 16, of which 8 were waited for; matrix products, arithmetic and copies ran while one was open for 1% of the time, Pallas kernels for 16%

profile of v3, /device:TPU:1, one launch (start us, length us, event | category | flops | bytes accessed | tf_op | source)
XLA Modules:
  0.0 104.1 jit_solution(11955045182671469482)
XLA Ops:
  0.0 2.5 %shard_map.37 = bf16[8,256,512]{2,1,0:T(8,128)(2,1)} custom-call(bf16[128,4096]{1,0:T(8,128)(2,1)} %occupied_ref.1, bf16[128,512]{1,0:T(8,128)(2,1)} %virtual_ref.1), custom_call_target="tpu_custom_call" | custom-call | bytes 4194304 | tf_op jit(solution)/shard_map/pallas_call | solution.py:194
  2.6 8.3 %all-to-all-start = ((bf16[8,256,512]{2,1,0:T(8,128)(2,1)}), bf16[8,256,512]{2,1,0:T(8,128)(2,1)S(1)}, u32[]{:S(2)}, u32[]{:S(2)}) async-start(bf16[8,256,512]{2,1,0:T(8,128)(2,1)} %shard_map.37), calls=%async_computation | async-start | bytes 4194304 | tf_op jit(solution)/shard_map/all_to_all | solution.py:207
  10.9 0.1 pad_add_fusion.place_ref
  11.0 4.1 %shard_map.38.amplitudes_ref = bf16[4096,1024]{1,0:T(8,128)(2,1)S(1)} custom-call(s32[4]{0:T(128)S(1)} %pad_add_fusion.place_ref, bf16[4096,2048]{1,0:T(8,128)(2,1)} %amplitudes_ref.3), custom_call_target="tpu_custom_call" | custom-call | bytes 16777216 | tf_op jit(solution)/shard_map/pallas_call | solution.py:209
  15.1 3.3 %copy-done = bf16[4096,1024]{1,0:T(8,128)(2,1)} copy-done((bf16[4096,1024]{1,0:T(8,128)(2,1)}, bf16[4096,1024]{1,0:T(8,128)(2,1)S(1)}, u32[]{:S(2)}) %copy-start) | copy-done | bytes 8388632
  18.4 18.7 %all-to-all-done.factors_ref = bf16[8,256,512]{2,1,0:T(8,128)(2,1)S(1)} async-done(((bf16[8,256,512]{2,1,0:T(8,128)(2,1)}), bf16[8,256,512]{2,1,0:T(8,128)(2,1)S(1)}, u32[]{:S(2)}, u32[]{:S(2)}) %all-to-all-start) | async-done | bytes 2097184 | tf_op jit(solution)/shard_map/all_to_all | solution.py:207
  37.0 1.3 %shard_map.39 = (f32[256,512]{1,0:T(8,128)S(1)}, f32[256,512]{1,0:T(8,128)S(1)}) custom-call(s32[4]{0:T(128)S(1)} %pad_add_fusion.place_ref, bf16[8,256,512]{2,1,0:T(8,128)(2,1)S(1)} %all-to-all-done.factors_ref), custom_call_target="tpu_custom_call" | custom-call | flops 536870912 | bytes 3145728 | tf_op jit(solution)/shard_map/pallas_call | solution.py:222
  38.4 1.3 %collective-permute-start = (f32[256,512]{1,0:T(8,128)S(1)}, f32[256,512]{1,0:T(8,128)S(1)}, u32[]{:S(2)}, u32[]{:S(2)}) collective-permute-start(f32[256,512]{1,0:T(8,128)S(1)} %get-tuple-element.19), channel_id=1, source_target_pairs={{0,8},{8,0},{16,24},{24,16},{32,40},{40,32},{48,56},{56,48},{64,72... | collective-permute-start | bytes 1572872 | tf_op jit(solution)/shard_map/ppermute | solution.py:231
  39.7 1.5 %collective-permute-done.came_ref = f32[256,512]{1,0:T(8,128)S(1)} collective-permute-done((f32[256,512]{1,0:T(8,128)S(1)}, f32[256,512]{1,0:T(8,128)S(1)}, u32[]{:S(2)}, u32[]{:S(2)}) %collective-permute-start) | collective-permute-done | bytes 524320 | tf_op jit(solution)/shard_map/ppermute | solution.py:231
  41.2 1.4 %shard_map.40.b0 = bf16[512,256]{1,0:T(8,128)(2,1)S(1)} custom-call(s32[4]{0:T(128)S(1)} %pad_add_fusion.place_ref, f32[256,512]{1,0:T(8,128)S(1)} %get-tuple-element.18.kept_ref, f32[256,512]{1,0:T(8,128)S(1)} %collective-permute-done.came_ref), custom_call_target="tpu_custom_call" | custom-call | flops 268435456 | bytes 2097152 | tf_op jit(solution)/shard_map/pallas_call | solution.py:232
  42.6 0.0 slice-start.1
  42.6 0.4 collective-permute-start.1
  43.0 2.9 %collective-permute-start.3 = (bf16[512,256]{1,0:T(8,128)(2,1)S(1)}, bf16[512,256]{1,0:T(8,128)(2,1)S(1)}, u32[]{:S(2)}, u32[]{:S(2)}) collective-permute-start(bf16[512,256]{1,0:T(8,128)(2,1)S(1)} %shard_map.40.b0), channel_id=1, source_target_pairs={{0,2},{1,3},{2,0},{3,1},{4,6},{5,7},{6,4},{7,5},{8,10},{9,11},{10,... | collective-permute-start | bytes 786440 | tf_op jit(solution)/shard_map/ppermute | solution.py:192
  45.9 0.4 collective-permute-start.6
  46.3 0.4 collective-permute-start.7
  46.7 4.1 %shard_map.41.held_ref = bf16[4096,1024]{1,0:T(8,128)(2,1)S(1)} custom-call(s32[4]{0:T(128)S(1)} %pad_add_fusion.place_ref, bf16[4096,2048]{1,0:T(8,128)(2,1)} %amplitudes_ref.3), custom_call_target="tpu_custom_call" | custom-call | bytes 16777216 | tf_op jit(solution)/shard_map/pallas_call | solution.py:209
  50.8 0.0 collective-permute-done.1.b0
  50.8 0.9 collective-permute-start.2
  51.8 1.9 %collective-permute-start.5 = (bf16[512,256]{1,0:T(8,128)(2,1)S(1)}, bf16[512,256]{1,0:T(8,128)(2,1)S(1)}, u32[]{:S(2)}, u32[]{:S(2)}) collective-permute-start(bf16[512,256]{1,0:T(8,128)(2,1)S(1)} %collective-permute-done.1.b0), channel_id=1, source_target_pairs={{0,3},{1,2},{2,1},{3,0},{4,7},{5,6},{6,5},{7,4},{8,11},{9,10},{10,... | collective-permute-start | bytes 786440 | tf_op jit(solution)/shard_map/ppermute | solution.py:192
  53.7 0.0 collective-permute-done.3.b2
  53.7 1.1 %collective-permute-start.4 = (bf16[512,256]{1,0:T(8,128)(2,1)S(1)}, bf16[512,256]{1,0:T(8,128)(2,1)S(1)}, u32[]{:S(2)}, u32[]{:S(2)}) collective-permute-start(bf16[512,256]{1,0:T(8,128)(2,1)S(1)} %collective-permute-done.3.b2), channel_id=1, source_target_pairs={{0,4},{1,5},{2,6},{3,7},{4,0},{5,1},{6,2},{7,3},{8,12},{9,13},{10,... | collective-permute-start | bytes 786440 | tf_op jit(solution)/shard_map/ppermute | solution.py:192
  54.8 2.9 %collective-permute-done.6.b1 = bf16[512,256]{1,0:T(8,128)(2,1)S(1)} collective-permute-done((bf16[512,256]{1,0:T(8,128)(2,1)S(1)}, bf16[512,256]{1,0:T(8,128)(2,1)S(1)}, u32[]{:S(2)}, u32[]{:S(2)}) %collective-permute-start.6) | collective-permute-done | bytes 262176 | tf_op jit(solution)/shard_map/ppermute | solution.py:192
  57.7 0.6 collective-permute-done.7.b3
  58.3 5.2 %shard_map.42.near_ref = f32[512,4096]{1,0:T(8,128)S(1)} custom-call(s32[4]{0:T(128)S(1)} %pad_add_fusion.place_ref, bf16[512,256]{1,0:T(8,128)(2,1)S(1)} %shard_map.40.b0, bf16[512,256]{1,0:T(8,128)(2,1)S(1)} %collective-permute-done.6.b1, bf16[512,256]{1,0:T(8,128)(2,1)S(1)} %collective-permute-done.3.b2, bf16[512,256]{1,0:T(8,128)(2,1)S(1)} %collective-permute-done.7.b3, ...), custom_call_target="tpu_custom_call" | custom-call | flops 4294967296 | bytes 17825792 | tf_op jit(solution)/shard_map/pallas_call | solution.py:253
  63.5 0.0 collective-permute-done.2.b1
  63.5 0.0 collective-permute-done.4.b2
  63.5 0.4 collective-permute-done.5.b3
  63.9 3.0 %shard_map.44 = (f32[128,4096]{1,0:T(8,128)S(1)}, bf16[128,4096]{1,0:T(8,128)(2,1)S(1)}) custom-call(s32[4]{0:T(128)S(1)} %pad_add_fusion.place_ref, bf16[512,256]{1,0:T(8,128)(2,1)S(1)} %collective-permute-done.1.b0, bf16[512,256]{1,0:T(8,128)(2,1)S(1)} %collective-permute-done.2.b1, bf16[512,256]{1,0:T(8,128)(2,1)S(1)} %collective-permute-done.4.b2, ...), custom_call_target="tpu_custom_call" | custom-call | flops 2147483648 | bytes 12582912 | tf_op jit(solution)/shard_map/pallas_call | solution.py:265
  66.9 1.7 %collective-permute-start.9 = (bf16[128,4096]{1,0:T(8,128)(2,1)S(1)}, bf16[128,4096]{1,0:T(8,128)(2,1)S(1)}, u32[]{:S(2)}, u32[]{:S(2)}) collective-permute-start(bf16[128,4096]{1,0:T(8,128)(2,1)S(1)} %get-tuple-element.25), channel_id=1, source_target_pairs={{0,8},{8,0},{16,24},{24,16},{32,40},{40,32},{48,56},{56,48},{64,72... | collective-permute-start | bytes 3145736 | tf_op jit(solution)/shard_map/ppermute | solution.py:287
  68.7 3.0 %shard_map.43 = (f32[128,4096]{1,0:T(8,128)S(1)}, bf16[128,4096]{1,0:T(8,128)(2,1)S(1)}) custom-call(s32[4]{0:T(128)S(1)} %pad_add_fusion.place_ref, bf16[512,256]{1,0:T(8,128)(2,1)S(1)} %collective-permute-done.1.b0, bf16[512,256]{1,0:T(8,128)(2,1)S(1)} %collective-permute-done.2.b1, bf16[512,256]{1,0:T(8,128)(2,1)S(1)} %collective-permute-done.4.b2, ...), custom_call_target="tpu_custom_call" | custom-call | flops 2147483648 | bytes 12582912 | tf_op jit(solution)/shard_map/pallas_call | solution.py:265
  71.6 0.1 collective-permute-start.8
  71.7 0.0 collective-permute-done.9
  71.7 0.2 add_convert_fusion
  72.0 0.1 fusion.3
  72.1 3.9 %collective-permute-start.10 = (bf16[64,4096]{1,0:T(8,128)(2,1)S(1)}, bf16[64,4096]{1,0:T(8,128)(2,1)S(1)}, u32[]{:S(2)}, u32[]{:S(2)}) collective-permute-start(bf16[64,4096]{1,0:T(8,128)(2,1)S(1)} %get-tuple-element.33), channel_id=1, source_target_pairs={{0,80},{8,120},{16,64},{24,104},{32,112},{40,88},{48,96},{56,72},{... | collective-permute-start | bytes 1572872 | tf_op jit(solution)/shard_map/ppermute | solution.py:283
  75.9 1.6 %collective-permute-start.11 = (bf16[64,4096]{1,0:T(8,128)(2,1)S(1)}, bf16[64,4096]{1,0:T(8,128)(2,1)S(1)}, u32[]{:S(2)}, u32[]{:S(2)}) collective-permute-start(bf16[64,4096]{1,0:T(8,128)(2,1)S(1)} %get-tuple-element.34), channel_id=1, source_target_pairs={{0,32},{8,104},{16,48},{24,120},{32,0},{40,72},{48,16},{56,88},{64... | collective-permute-start | bytes 1572872 | tf_op jit(solution)/shard_map/ppermute | solution.py:283
  77.5 0.0 collective-permute-done.8
  77.5 0.3 fusion.2
  77.9 2.3 %collective-permute-start.12 = (bf16[32,4096]{1,0:T(8,128)(2,1)S(1)}, bf16[32,4096]{1,0:T(8,128)(2,1)S(1)}, u32[]{:S(2)}, u32[]{:S(2)}) collective-permute-start(bf16[32,4096]{1,0:T(8,128)(2,1)S(1)} %slice.53), channel_id=1, source_target_pairs={{0,64},{8,72},{16,80},{24,88},{32,96},{40,104},{48,112},{56,120},{... | collective-permute-start | bytes 786440 | tf_op jit(solution)/shard_map/ppermute | solution.py:283
  80.3 0.5 collective-permute-start.13
  80.7 19.7 %collective-permute-done.12 = bf16[32,4096]{1,0:T(8,128)(2,1)S(1)} collective-permute-done((bf16[32,4096]{1,0:T(8,128)(2,1)S(1)}, bf16[32,4096]{1,0:T(8,128)(2,1)S(1)}, u32[]{:S(2)}, u32[]{:S(2)}) %collective-permute-start.12) | collective-permute-done | bytes 262176 | tf_op jit(solution)/shard_map/ppermute | solution.py:283
  100.4 0.0 collective-permute-done.10
  100.4 0.0 collective-permute-done.11
  100.5 0.2 convert_add_fusion.2
  100.6 0.5 collective-permute-done.13
  101.2 0.3 collective-permute-start.14
  101.5 1.7 %collective-permute-done.14 = f32[32,4096]{1,0:T(8,128)S(1)} collective-permute-done((f32[32,4096]{1,0:T(8,128)S(1)}, f32[32,4096]{1,0:T(8,128)S(1)}, u32[]{:S(2)}, u32[]{:S(2)}) %collective-permute-start.14) | collective-permute-done | bytes 524320 | tf_op jit(solution)/shard_map/ppermute | solution.py:297
  103.2 0.9 add_bitcast_fusion
  (8 shorter events, 0.1 us)
Async XLA Ops:
  2.6 34.5 %all-to-all-start = ((bf16[8,256,512]{2,1,0:T(8,128)(2,1)}), bf16[8,256,512]{2,1,0:T(8,128)(2,1)S(1)}, u32[]{:S(2)}, u32[]{:S(2)}) async-start(bf16[8,256,512]{2,1,0:T(8,128)(2,1)} %shard_map.37), calls=%async_computation | async-start | bytes 4194304 | tf_op jit(solution)/shard_map/all_to_all | solution.py:207
  15.1 3.3 %copy-start = (bf16[4096,1024]{1,0:T(8,128)(2,1)}, bf16[4096,1024]{1,0:T(8,128)(2,1)S(1)}, u32[]{:S(2)}) copy-start(bf16[4096,1024]{1,0:T(8,128)(2,1)S(1)} %shard_map.38.amplitudes_ref) | copy-start | bytes 25165828
  38.4 2.8 %collective-permute-start = (f32[256,512]{1,0:T(8,128)S(1)}, f32[256,512]{1,0:T(8,128)S(1)}, u32[]{:S(2)}, u32[]{:S(2)}) collective-permute-start(f32[256,512]{1,0:T(8,128)S(1)} %get-tuple-element.19), channel_id=1, source_target_pairs={{0,8},{8,0},{16,24},{24,16},{32,40},{40,32},{48,56},{56,48},{64,72... | collective-permute-start | bytes 1572872 | tf_op jit(solution)/shard_map/ppermute | solution.py:231
  41.2 22.7 %slice-start = ((s8[8388608]{0:T(1024)(128)(4,1)}), s8[4194304]{0:T(1024)(128)(4,1)S(1)}, s32[]{:S(2)}) async-start(s8[8388608]{0:T(1024)(128)(4,1)} %bitcast.6), calls=%async_computation.1 | async-start | bytes 8388608
  42.6 21.4 %slice-start.1 = ((s8[8388608]{0:T(1024)(128)(4,1)}), s8[4194304]{0:T(1024)(128)(4,1)S(1)}, s32[]{:S(2)}) async-start(s8[8388608]{0:T(1024)(128)(4,1)} %bitcast.6), calls=%async_computation.2 | async-start | bytes 8388608
  42.6 8.2 %collective-permute-start.1 = (bf16[512,256]{1,0:T(8,128)(2,1)S(1)}, bf16[512,256]{1,0:T(8,128)(2,1)S(1)}, u32[]{:S(2)}, u32[]{:S(2)}) collective-permute-start(bf16[512,256]{1,0:T(8,128)(2,1)S(1)} %shard_map.40.b0), channel_id=1, source_target_pairs={{0,4},{1,5},{2,6},{3,7},{4,0},{5,1},{6,2},{7,3},{8,12},{9,13},{10,... | collective-permute-start | bytes 786440 | tf_op jit(solution)/shard_map/ppermute | solution.py:192
  43.0 10.7 %collective-permute-start.3 = (bf16[512,256]{1,0:T(8,128)(2,1)S(1)}, bf16[512,256]{1,0:T(8,128)(2,1)S(1)}, u32[]{:S(2)}, u32[]{:S(2)}) collective-permute-start(bf16[512,256]{1,0:T(8,128)(2,1)S(1)} %shard_map.40.b0), channel_id=1, source_target_pairs={{0,2},{1,3},{2,0},{3,1},{4,6},{5,7},{6,4},{7,5},{8,10},{9,11},{10,... | collective-permute-start | bytes 786440 | tf_op jit(solution)/shard_map/ppermute | solution.py:192
  45.9 11.8 %collective-permute-start.6 = (bf16[512,256]{1,0:T(8,128)(2,1)S(1)}, bf16[512,256]{1,0:T(8,128)(2,1)S(1)}, u32[]{:S(2)}, u32[]{:S(2)}) collective-permute-start(bf16[512,256]{1,0:T(8,128)(2,1)S(1)} %shard_map.40.b0), channel_id=1, source_target_pairs={{0,1},{1,0},{2,3},{3,2},{4,5},{5,4},{6,7},{7,6},{8,9},{9,8},{10,11... | collective-permute-start | bytes 786440 | tf_op jit(solution)/shard_map/ppermute | solution.py:192
  46.3 12.0 %collective-permute-start.7 = (bf16[512,256]{1,0:T(8,128)(2,1)S(1)}, bf16[512,256]{1,0:T(8,128)(2,1)S(1)}, u32[]{:S(2)}, u32[]{:S(2)}) collective-permute-start(bf16[512,256]{1,0:T(8,128)(2,1)S(1)} %shard_map.40.b0), channel_id=1, source_target_pairs={{0,3},{1,2},{2,1},{3,0},{4,7},{5,6},{6,5},{7,4},{8,11},{9,10},{10,... | collective-permute-start | bytes 786440 | tf_op jit(solution)/shard_map/ppermute | solution.py:192
  50.8 12.7 %collective-permute-start.2 = (bf16[512,256]{1,0:T(8,128)(2,1)S(1)}, bf16[512,256]{1,0:T(8,128)(2,1)S(1)}, u32[]{:S(2)}, u32[]{:S(2)}) collective-permute-start(bf16[512,256]{1,0:T(8,128)(2,1)S(1)} %collective-permute-done.1.b0), channel_id=1, source_target_pairs={{0,1},{1,0},{2,3},{3,2},{4,5},{5,4},{6,7},{7,6},{8,9},{9,8},{10,11... | collective-permute-start | bytes 786440 | tf_op jit(solution)/shard_map/ppermute | solution.py:192
  51.8 12.2 %collective-permute-start.5 = (bf16[512,256]{1,0:T(8,128)(2,1)S(1)}, bf16[512,256]{1,0:T(8,128)(2,1)S(1)}, u32[]{:S(2)}, u32[]{:S(2)}) collective-permute-start(bf16[512,256]{1,0:T(8,128)(2,1)S(1)} %collective-permute-done.1.b0), channel_id=1, source_target_pairs={{0,3},{1,2},{2,1},{3,0},{4,7},{5,6},{6,5},{7,4},{8,11},{9,10},{10,... | collective-permute-start | bytes 786440 | tf_op jit(solution)/shard_map/ppermute | solution.py:192
  53.7 9.8 %collective-permute-start.4 = (bf16[512,256]{1,0:T(8,128)(2,1)S(1)}, bf16[512,256]{1,0:T(8,128)(2,1)S(1)}, u32[]{:S(2)}, u32[]{:S(2)}) collective-permute-start(bf16[512,256]{1,0:T(8,128)(2,1)S(1)} %collective-permute-done.3.b2), channel_id=1, source_target_pairs={{0,4},{1,5},{2,6},{3,7},{4,0},{5,1},{6,2},{7,3},{8,12},{9,13},{10,... | collective-permute-start | bytes 786440 | tf_op jit(solution)/shard_map/ppermute | solution.py:192
  66.9 4.8 %collective-permute-start.9 = (bf16[128,4096]{1,0:T(8,128)(2,1)S(1)}, bf16[128,4096]{1,0:T(8,128)(2,1)S(1)}, u32[]{:S(2)}, u32[]{:S(2)}) collective-permute-start(bf16[128,4096]{1,0:T(8,128)(2,1)S(1)} %get-tuple-element.25), channel_id=1, source_target_pairs={{0,8},{8,0},{16,24},{24,16},{32,40},{40,32},{48,56},{56,48},{64,72... | collective-permute-start | bytes 3145736 | tf_op jit(solution)/shard_map/ppermute | solution.py:287
  71.6 5.9 %collective-permute-start.8 = (bf16[128,4096]{1,0:T(8,128)(2,1)S(1)}, bf16[128,4096]{1,0:T(8,128)(2,1)S(1)}, u32[]{:S(2)}, u32[]{:S(2)}) collective-permute-start(bf16[128,4096]{1,0:T(8,128)(2,1)S(1)} %get-tuple-element.23), channel_id=1, source_target_pairs={{0,8},{8,0},{16,24},{24,16},{32,40},{40,32},{48,56},{56,48},{64,72... | collective-permute-start | bytes 3145736 | tf_op jit(solution)/shard_map/ppermute | solution.py:290
  72.1 28.4 %collective-permute-start.10 = (bf16[64,4096]{1,0:T(8,128)(2,1)S(1)}, bf16[64,4096]{1,0:T(8,128)(2,1)S(1)}, u32[]{:S(2)}, u32[]{:S(2)}) collective-permute-start(bf16[64,4096]{1,0:T(8,128)(2,1)S(1)} %get-tuple-element.33), channel_id=1, source_target_pairs={{0,80},{8,120},{16,64},{24,104},{32,112},{40,88},{48,96},{56,72},{... | collective-permute-start | bytes 1572872 | tf_op jit(solution)/shard_map/ppermute | solution.py:283
  75.9 24.5 %collective-permute-start.11 = (bf16[64,4096]{1,0:T(8,128)(2,1)S(1)}, bf16[64,4096]{1,0:T(8,128)(2,1)S(1)}, u32[]{:S(2)}, u32[]{:S(2)}) collective-permute-start(bf16[64,4096]{1,0:T(8,128)(2,1)S(1)} %get-tuple-element.34), channel_id=1, source_target_pairs={{0,32},{8,104},{16,48},{24,120},{32,0},{40,72},{48,16},{56,88},{64... | collective-permute-start | bytes 1572872 | tf_op jit(solution)/shard_map/ppermute | solution.py:283
  77.9 22.5 %collective-permute-start.12 = (bf16[32,4096]{1,0:T(8,128)(2,1)S(1)}, bf16[32,4096]{1,0:T(8,128)(2,1)S(1)}, u32[]{:S(2)}, u32[]{:S(2)}) collective-permute-start(bf16[32,4096]{1,0:T(8,128)(2,1)S(1)} %slice.53), channel_id=1, source_target_pairs={{0,64},{8,72},{16,80},{24,88},{32,96},{40,104},{48,112},{56,120},{... | collective-permute-start | bytes 786440 | tf_op jit(solution)/shard_map/ppermute | solution.py:283
  80.3 20.9 %collective-permute-start.13 = (bf16[64,4096]{1,0:T(8,128)(2,1)S(1)}, bf16[64,4096]{1,0:T(8,128)(2,1)S(1)}, u32[]{:S(2)}, u32[]{:S(2)}) collective-permute-start(bf16[64,4096]{1,0:T(8,128)(2,1)S(1)} %slice.56), channel_id=1, source_target_pairs={{0,16},{8,56},{16,0},{24,40},{32,48},{40,24},{48,32},{56,8},{64,80... | collective-permute-start | bytes 1572872 | tf_op jit(solution)/shard_map/ppermute | solution.py:283
  101.2 2.0 %collective-permute-start.14 = (f32[32,4096]{1,0:T(8,128)S(1)}, f32[32,4096]{1,0:T(8,128)S(1)}, u32[]{:S(2)}, u32[]{:S(2)}) collective-permute-start(f32[32,4096]{1,0:T(8,128)S(1)} %convert_add_fusion.1), channel_id=1, source_target_pairs={{0,8},{8,0},{16,24},{24,16},{32,40},{40,32},{48,56},{56,48},{64,72... | collective-permute-start | bytes 1572872 | tf_op jit(solution)/shard_map/ppermute | solution.py:297

commit v4 on v3

--- a/solution.py
+++ b/solution.py
@@ -59,18 +59,16 @@
         copy.wait()
 
 
-def integrals_kernel(place_ref, factors_ref, kept_ref, sent_ref, total):
+def integrals_kernel(other, place_ref, factors_ref, out_ref):
     sources, two_depth, cb = factors_ref.shape
     depth = two_depth // 2
-    half = kept_ref.shape[0]
-    occupied = factors_ref[:, :depth].reshape(sources * depth, cb)
+    half = out_ref.shape[0]
+    at = pl.multiple_of((place_ref[1] ^ other) * half, half)
+    occupied = factors_ref[:, :depth, pl.ds(at, half)].reshape(sources * depth, half)
     virtual = factors_ref[:, depth:].reshape(sources * depth, cb)
-    total[...] = lax.dot_general(
+    out_ref[...] = lax.dot_general(
         occupied, virtual, (((0,), (0,)), ((), ())), preferred_element_type=F32
     )
-    core = place_ref[1]
-    kept_ref[...] = total[pl.ds(pl.multiple_of(core * half, half), half), :]
-    sent_ref[...] = total[pl.ds(pl.multiple_of((1 - core) * half, half), half), :]
 
 
 def block_kernel(place_ref, kept_ref, came_ref, out_ref):
@@ -80,7 +78,7 @@
     rows = O * BW
     integrals = (kept_ref[...] + came_ref[...]).astype(BF16)
     source = lax.broadcasted_iota(jnp.int32, (cb, cb), 0)
-    target = lax.broadcasted_iota(jnp.int32, (cb, cb), 1)
+    target = lax.broadcasted_iota(jnp.int32, (1, cb), 1)
     move = jnp.where(source == (target % cs) * BW + target // cs, 1.0, 0.0).astype(BF16)
     by_b = jnp.dot(integrals, move, preferred_element_type=F32).astype(BF16)
     stacked = jnp.concatenate(
@@ -219,15 +217,17 @@
     held_far = columns(1, place)
     factors, held_far = lax.optimization_barrier((factors, held_far))
     half = jax.ShapeDtypeStruct((kj // kc_size, cb), F32)
-    kept, sent = call(
-        integrals_kernel,
-        (half, half),
-        1,
-        1,
-        scratch=[pltpu.VMEM((kj // chips, cb), F32)],
-        flops=2 * chips * depth * cb * cb,
-        moved=3 * MIB,
-    )(place, factors)
+    sent, kept = (
+        call(
+            functools.partial(integrals_kernel, other),
+            half,
+            1,
+            1,
+            flops=chips * depth * cb * cb,
+            moved=3 * MIB,
+        )(place, factors)
+        for other in (1, 0)
+    )
     came = lax.ppermute(sent, "kc", swap)
     own = call(
         block_kernel,

time: 104 us -> 104 us (level)
  transfers between devices with their start and end apart: 16 -> 16, of which waited for: 8 -> 8; matrix products, arithmetic and copies ran while one was open for 1% -> 1% of each run, Pallas kernels for 16% -> 17%
where the time goes in v4:
time: 104 us
  waiting for transfers between devices  45.1 us (43%)
  starting transfers between devices  28.1 us (27%)
  Pallas kernels  25.3 us (24%)
  local copies, waits for them, and re-layouts  3.42 us (3%)
  other arithmetic  1.66 us (2%)
    ppermute x4, waiting for transfers between devices, to_slot(): return lax.ppermute(array, 'kc', pairs)  20.3 us
    all_to_all x1, waiting for transfers between devices, per_device(): factors = lax.all_to_all(payload, 'kc', 0, 0, axis_index_groups=same_core)  18.7 us
    all_to_all x1, starting transfers between devices, per_device(): factors = lax.all_to_all(payload, 'kc', 0, 0, axis_index_groups=same_core)  8.34 us
    ppermute x4, starting transfers between devices, to_slot(): return lax.ppermute(array, 'kc', pairs)  8.28 us
    pallas_call x2, Pallas kernels, columns(): pl.pallas_call(functools.partial(columns_kernel, far), out_shape=jax.Shap...  8.26 us
    ppermute x7, starting transfers between devices, over_ia(): return lax.ppermute(array, 'ia', [(i, i ^ bits) for i in range(ia_size)])  8.07 us
    pallas_call x2, Pallas kernels, far(): call(functools.partial(far_kernel, tile, lo), (jax.ShapeDtypeStruct((part...  5.95 us
    pallas_call x1, Pallas kernels, per_device(): call(functools.partial(near_kernel, tile), jax.ShapeDtypeStruct((rows, lo...  5.17 us
  transfers between devices with their start and end apart: 16, of which 8 were waited for; matrix products, arithmetic and copies ran while one was open for 1% of the time, Pallas kernels for 17%

profile of v4, /device:TPU:1, one launch (start us, length us, event | category | flops | bytes accessed | tf_op | source)
XLA Modules:
  0.0 103.7 jit_solution(18434751432555928059)
XLA Ops:
  0.0 2.5 %shard_map.37 = bf16[8,256,512]{2,1,0:T(8,128)(2,1)} custom-call(bf16[128,4096]{1,0:T(8,128)(2,1)} %occupied_ref.1, bf16[128,512]{1,0:T(8,128)(2,1)} %virtual_ref.1), custom_call_target="tpu_custom_call" | custom-call | bytes 4194304 | tf_op jit(solution)/shard_map/pallas_call | solution.py:192
  2.5 8.3 %all-to-all-start = ((bf16[8,256,512]{2,1,0:T(8,128)(2,1)}), bf16[8,256,512]{2,1,0:T(8,128)(2,1)S(1)}, u32[]{:S(2)}, u32[]{:S(2)}) async-start(bf16[8,256,512]{2,1,0:T(8,128)(2,1)} %shard_map.37), calls=%async_computation | async-start | bytes 4194304 | tf_op jit(solution)/shard_map/all_to_all | solution.py:205
  10.9 0.1 pad_add_fusion.place_ref
  11.0 4.1 %shard_map.38.amplitudes_ref = bf16[4096,1024]{1,0:T(8,128)(2,1)S(1)} custom-call(s32[4]{0:T(128)S(1)} %pad_add_fusion.place_ref, bf16[4096,2048]{1,0:T(8,128)(2,1)} %amplitudes_ref.3), custom_call_target="tpu_custom_call" | custom-call | bytes 16777216 | tf_op jit(solution)/shard_map/pallas_call | solution.py:207
  15.1 3.3 %copy-done = bf16[4096,1024]{1,0:T(8,128)(2,1)} copy-done((bf16[4096,1024]{1,0:T(8,128)(2,1)}, bf16[4096,1024]{1,0:T(8,128)(2,1)S(1)}, u32[]{:S(2)}) %copy-start) | copy-done | bytes 8388632
  18.4 18.7 %all-to-all-done.factors_ref = bf16[8,256,512]{2,1,0:T(8,128)(2,1)S(1)} async-done(((bf16[8,256,512]{2,1,0:T(8,128)(2,1)}), bf16[8,256,512]{2,1,0:T(8,128)(2,1)S(1)}, u32[]{:S(2)}, u32[]{:S(2)}) %all-to-all-start) | async-done | bytes 2097184 | tf_op jit(solution)/shard_map/all_to_all | solution.py:205
  37.0 1.0 shard_map.40
  38.0 1.3 %collective-permute-start = (f32[256,512]{1,0:T(8,128)S(1)}, f32[256,512]{1,0:T(8,128)S(1)}, u32[]{:S(2)}, u32[]{:S(2)}) collective-permute-start(f32[256,512]{1,0:T(8,128)S(1)} %shard_map.40), channel_id=1, source_target_pairs={{0,8},{8,0},{16,24},{24,16},{32,40},{40,32},{48,56},{56,48},{64,72... | collective-permute-start | bytes 1572872 | tf_op jit(solution)/shard_map/ppermute | solution.py:231
  39.3 1.0 shard_map.39.kept_ref
  40.4 0.5 collective-permute-done.came_ref
  40.9 1.4 %shard_map.41.b0 = bf16[512,256]{1,0:T(8,128)(2,1)S(1)} custom-call(s32[4]{0:T(128)S(1)} %pad_add_fusion.place_ref, f32[256,512]{1,0:T(8,128)S(1)} %shard_map.39.kept_ref, f32[256,512]{1,0:T(8,128)S(1)} %collective-permute-done.came_ref), custom_call_target="tpu_custom_call" | custom-call | flops 268435456 | bytes 2097152 | tf_op jit(solution)/shard_map/pallas_call | solution.py:232
  42.2 0.0 slice-start.1
  42.3 0.4 collective-permute-start.1
  42.6 2.9 %collective-permute-start.3 = (bf16[512,256]{1,0:T(8,128)(2,1)S(1)}, bf16[512,256]{1,0:T(8,128)(2,1)S(1)}, u32[]{:S(2)}, u32[]{:S(2)}) collective-permute-start(bf16[512,256]{1,0:T(8,128)(2,1)S(1)} %shard_map.41.b0), channel_id=1, source_target_pairs={{0,2},{1,3},{2,0},{3,1},{4,6},{5,7},{6,4},{7,5},{8,10},{9,11},{10,... | collective-permute-start | bytes 786440 | tf_op jit(solution)/shard_map/ppermute | solution.py:190
  45.6 0.4 collective-permute-start.6
  46.0 0.4 collective-permute-start.7
  46.3 4.1 %shard_map.42.held_ref = bf16[4096,1024]{1,0:T(8,128)(2,1)S(1)} custom-call(s32[4]{0:T(128)S(1)} %pad_add_fusion.place_ref, bf16[4096,2048]{1,0:T(8,128)(2,1)} %amplitudes_ref.3), custom_call_target="tpu_custom_call" | custom-call | bytes 16777216 | tf_op jit(solution)/shard_map/pallas_call | solution.py:207
  50.5 0.0 collective-permute-done.1.b0
  50.5 0.9 collective-permute-start.2
  51.4 1.9 %collective-permute-start.5 = (bf16[512,256]{1,0:T(8,128)(2,1)S(1)}, bf16[512,256]{1,0:T(8,128)(2,1)S(1)}, u32[]{:S(2)}, u32[]{:S(2)}) collective-permute-start(bf16[512,256]{1,0:T(8,128)(2,1)S(1)} %collective-permute-done.1.b0), channel_id=1, source_target_pairs={{0,3},{1,2},{2,1},{3,0},{4,7},{5,6},{6,5},{7,4},{8,11},{9,10},{10,... | collective-permute-start | bytes 786440 | tf_op jit(solution)/shard_map/ppermute | solution.py:190
  53.3 0.0 collective-permute-done.3.b2
  53.3 1.1 %collective-permute-start.4 = (bf16[512,256]{1,0:T(8,128)(2,1)S(1)}, bf16[512,256]{1,0:T(8,128)(2,1)S(1)}, u32[]{:S(2)}, u32[]{:S(2)}) collective-permute-start(bf16[512,256]{1,0:T(8,128)(2,1)S(1)} %collective-permute-done.3.b2), channel_id=1, source_target_pairs={{0,4},{1,5},{2,6},{3,7},{4,0},{5,1},{6,2},{7,3},{8,12},{9,13},{10,... | collective-permute-start | bytes 786440 | tf_op jit(solution)/shard_map/ppermute | solution.py:190
  54.5 2.9 %collective-permute-done.6.b1 = bf16[512,256]{1,0:T(8,128)(2,1)S(1)} collective-permute-done((bf16[512,256]{1,0:T(8,128)(2,1)S(1)}, bf16[512,256]{1,0:T(8,128)(2,1)S(1)}, u32[]{:S(2)}, u32[]{:S(2)}) %collective-permute-start.6) | collective-permute-done | bytes 262176 | tf_op jit(solution)/shard_map/ppermute | solution.py:190
  57.3 0.6 collective-permute-done.7.b3
  58.0 5.2 %shard_map.43.near_ref = f32[512,4096]{1,0:T(8,128)S(1)} custom-call(s32[4]{0:T(128)S(1)} %pad_add_fusion.place_ref, bf16[512,256]{1,0:T(8,128)(2,1)S(1)} %shard_map.41.b0, bf16[512,256]{1,0:T(8,128)(2,1)S(1)} %collective-permute-done.6.b1, bf16[512,256]{1,0:T(8,128)(2,1)S(1)} %collective-permute-done.3.b2, bf16[512,256]{1,0:T(8,128)(2,1)S(1)} %collective-permute-done.7.b3, ...), custom_call_target="tpu_custom_call" | custom-call | flops 4294967296 | bytes 17825792 | tf_op jit(solution)/shard_map/pallas_call | solution.py:253
  63.2 0.0 collective-permute-done.2.b1
  63.2 0.0 collective-permute-done.4.b2
  63.2 0.4 collective-permute-done.5.b3
  63.6 3.0 %shard_map.45 = (f32[128,4096]{1,0:T(8,128)S(1)}, bf16[128,4096]{1,0:T(8,128)(2,1)S(1)}) custom-call(s32[4]{0:T(128)S(1)} %pad_add_fusion.place_ref, bf16[512,256]{1,0:T(8,128)(2,1)S(1)} %collective-permute-done.1.b0, bf16[512,256]{1,0:T(8,128)(2,1)S(1)} %collective-permute-done.2.b1, bf16[512,256]{1,0:T(8,128)(2,1)S(1)} %collective-permute-done.4.b2, ...), custom_call_target="tpu_custom_call" | custom-call | flops 2147483648 | bytes 12582912 | tf_op jit(solution)/shard_map/pallas_call | solution.py:265
  66.6 1.7 %collective-permute-start.9 = (bf16[128,4096]{1,0:T(8,128)(2,1)S(1)}, bf16[128,4096]{1,0:T(8,128)(2,1)S(1)}, u32[]{:S(2)}, u32[]{:S(2)}) collective-permute-start(bf16[128,4096]{1,0:T(8,128)(2,1)S(1)} %get-tuple-element.21), channel_id=1, source_target_pairs={{0,8},{8,0},{16,24},{24,16},{32,40},{40,32},{48,56},{56,48},{64,72... | collective-permute-start | bytes 3145736 | tf_op jit(solution)/shard_map/ppermute | solution.py:287
  68.3 3.0 %shard_map.44 = (f32[128,4096]{1,0:T(8,128)S(1)}, bf16[128,4096]{1,0:T(8,128)(2,1)S(1)}) custom-call(s32[4]{0:T(128)S(1)} %pad_add_fusion.place_ref, bf16[512,256]{1,0:T(8,128)(2,1)S(1)} %collective-permute-done.1.b0, bf16[512,256]{1,0:T(8,128)(2,1)S(1)} %collective-permute-done.2.b1, bf16[512,256]{1,0:T(8,128)(2,1)S(1)} %collective-permute-done.4.b2, ...), custom_call_target="tpu_custom_call" | custom-call | flops 2147483648 | bytes 12582912 | tf_op jit(solution)/shard_map/pallas_call | solution.py:265
  71.3 0.1 collective-permute-start.8
  71.4 0.0 collective-permute-done.9
  71.4 0.2 add_convert_fusion
  71.6 0.1 fusion.3
  71.7 3.9 %collective-permute-start.10 = (bf16[64,4096]{1,0:T(8,128)(2,1)S(1)}, bf16[64,4096]{1,0:T(8,128)(2,1)S(1)}, u32[]{:S(2)}, u32[]{:S(2)}) collective-permute-start(bf16[64,4096]{1,0:T(8,128)(2,1)S(1)} %get-tuple-element.29), channel_id=1, source_target_pairs={{0,80},{8,120},{16,64},{24,104},{32,112},{40,88},{48,96},{56,72},{... | collective-permute-start | bytes 1572872 | tf_op jit(solution)/shard_map/ppermute | solution.py:283
  75.6 1.6 %collective-permute-start.11 = (bf16[64,4096]{1,0:T(8,128)(2,1)S(1)}, bf16[64,4096]{1,0:T(8,128)(2,1)S(1)}, u32[]{:S(2)}, u32[]{:S(2)}) collective-permute-start(bf16[64,4096]{1,0:T(8,128)(2,1)S(1)} %get-tuple-element.30), channel_id=1, source_target_pairs={{0,32},{8,104},{16,48},{24,120},{32,0},{40,72},{48,16},{56,88},{64... | collective-permute-start | bytes 1572872 | tf_op jit(solution)/shard_map/ppermute | solution.py:283
  77.2 0.3 fusion.2
  77.6 2.3 %collective-permute-start.12 = (bf16[32,4096]{1,0:T(8,128)(2,1)S(1)}, bf16[32,4096]{1,0:T(8,128)(2,1)S(1)}, u32[]{:S(2)}, u32[]{:S(2)}) collective-permute-start(bf16[32,4096]{1,0:T(8,128)(2,1)S(1)} %slice.53), channel_id=1, source_target_pairs={{0,64},{8,72},{16,80},{24,88},{32,96},{40,104},{48,112},{56,120},{... | collective-permute-start | bytes 786440 | tf_op jit(solution)/shard_map/ppermute | solution.py:283
  79.9 0.4 collective-permute-start.13
  80.4 19.7 %collective-permute-done.12 = bf16[32,4096]{1,0:T(8,128)(2,1)S(1)} collective-permute-done((bf16[32,4096]{1,0:T(8,128)(2,1)S(1)}, bf16[32,4096]{1,0:T(8,128)(2,1)S(1)}, u32[]{:S(2)}, u32[]{:S(2)}) %collective-permute-start.12) | collective-permute-done | bytes 262176 | tf_op jit(solution)/shard_map/ppermute | solution.py:283
  100.1 0.0 collective-permute-done.10
  100.1 0.0 collective-permute-done.11
  100.1 0.2 convert_add_fusion.2
  100.3 0.5 collective-permute-done.13
  100.9 0.3 collective-permute-start.14
  101.1 1.7 %collective-permute-done.14 = f32[32,4096]{1,0:T(8,128)S(1)} collective-permute-done((f32[32,4096]{1,0:T(8,128)S(1)}, f32[32,4096]{1,0:T(8,128)S(1)}, u32[]{:S(2)}, u32[]{:S(2)}) %collective-permute-start.14) | collective-permute-done | bytes 524320 | tf_op jit(solution)/shard_map/ppermute | solution.py:297
  102.9 0.9 add_bitcast_fusion
  (9 shorter events, 0.1 us)
Async XLA Ops:
  2.5 34.5 %all-to-all-start = ((bf16[8,256,512]{2,1,0:T(8,128)(2,1)}), bf16[8,256,512]{2,1,0:T(8,128)(2,1)S(1)}, u32[]{:S(2)}, u32[]{:S(2)}) async-start(bf16[8,256,512]{2,1,0:T(8,128)(2,1)} %shard_map.37), calls=%async_computation | async-start | bytes 4194304 | tf_op jit(solution)/shard_map/all_to_all | solution.py:205
  15.1 3.3 %copy-start = (bf16[4096,1024]{1,0:T(8,128)(2,1)}, bf16[4096,1024]{1,0:T(8,128)(2,1)S(1)}, u32[]{:S(2)}) copy-start(bf16[4096,1024]{1,0:T(8,128)(2,1)S(1)} %shard_map.38.amplitudes_ref) | copy-start | bytes 25165828
  38.0 2.9 %collective-permute-start = (f32[256,512]{1,0:T(8,128)S(1)}, f32[256,512]{1,0:T(8,128)S(1)}, u32[]{:S(2)}, u32[]{:S(2)}) collective-permute-start(f32[256,512]{1,0:T(8,128)S(1)} %shard_map.40), channel_id=1, source_target_pairs={{0,8},{8,0},{16,24},{24,16},{32,40},{40,32},{48,56},{56,48},{64,72... | collective-permute-start | bytes 1572872 | tf_op jit(solution)/shard_map/ppermute | solution.py:231
  40.9 22.7 %slice-start = ((s8[8388608]{0:T(1024)(128)(4,1)}), s8[4194304]{0:T(1024)(128)(4,1)S(1)}, s32[]{:S(2)}) async-start(s8[8388608]{0:T(1024)(128)(4,1)} %bitcast.6), calls=%async_computation.1 | async-start | bytes 8388608
  42.2 21.4 %slice-start.1 = ((s8[8388608]{0:T(1024)(128)(4,1)}), s8[4194304]{0:T(1024)(128)(4,1)S(1)}, s32[]{:S(2)}) async-start(s8[8388608]{0:T(1024)(128)(4,1)} %bitcast.6), calls=%async_computation.2 | async-start | bytes 8388608
  42.3 8.2 %collective-permute-start.1 = (bf16[512,256]{1,0:T(8,128)(2,1)S(1)}, bf16[512,256]{1,0:T(8,128)(2,1)S(1)}, u32[]{:S(2)}, u32[]{:S(2)}) collective-permute-start(bf16[512,256]{1,0:T(8,128)(2,1)S(1)} %shard_map.41.b0), channel_id=1, source_target_pairs={{0,4},{1,5},{2,6},{3,7},{4,0},{5,1},{6,2},{7,3},{8,12},{9,13},{10,... | collective-permute-start | bytes 786440 | tf_op jit(solution)/shard_map/ppermute | solution.py:190
  42.6 10.7 %collective-permute-start.3 = (bf16[512,256]{1,0:T(8,128)(2,1)S(1)}, bf16[512,256]{1,0:T(8,128)(2,1)S(1)}, u32[]{:S(2)}, u32[]{:S(2)}) collective-permute-start(bf16[512,256]{1,0:T(8,128)(2,1)S(1)} %shard_map.41.b0), channel_id=1, source_target_pairs={{0,2},{1,3},{2,0},{3,1},{4,6},{5,7},{6,4},{7,5},{8,10},{9,11},{10,... | collective-permute-start | bytes 786440 | tf_op jit(solution)/shard_map/ppermute | solution.py:190
  45.6 11.8 %collective-permute-start.6 = (bf16[512,256]{1,0:T(8,128)(2,1)S(1)}, bf16[512,256]{1,0:T(8,128)(2,1)S(1)}, u32[]{:S(2)}, u32[]{:S(2)}) collective-permute-start(bf16[512,256]{1,0:T(8,128)(2,1)S(1)} %shard_map.41.b0), channel_id=1, source_target_pairs={{0,1},{1,0},{2,3},{3,2},{4,5},{5,4},{6,7},{7,6},{8,9},{9,8},{10,11... | collective-permute-start | bytes 786440 | tf_op jit(solution)/shard_map/ppermute | solution.py:190
  46.0 12.0 %collective-permute-start.7 = (bf16[512,256]{1,0:T(8,128)(2,1)S(1)}, bf16[512,256]{1,0:T(8,128)(2,1)S(1)}, u32[]{:S(2)}, u32[]{:S(2)}) collective-permute-start(bf16[512,256]{1,0:T(8,128)(2,1)S(1)} %shard_map.41.b0), channel_id=1, source_target_pairs={{0,3},{1,2},{2,1},{3,0},{4,7},{5,6},{6,5},{7,4},{8,11},{9,10},{10,... | collective-permute-start | bytes 786440 | tf_op jit(solution)/shard_map/ppermute | solution.py:190
  50.5 12.7 %collective-permute-start.2 = (bf16[512,256]{1,0:T(8,128)(2,1)S(1)}, bf16[512,256]{1,0:T(8,128)(2,1)S(1)}, u32[]{:S(2)}, u32[]{:S(2)}) collective-permute-start(bf16[512,256]{1,0:T(8,128)(2,1)S(1)} %collective-permute-done.1.b0), channel_id=1, source_target_pairs={{0,1},{1,0},{2,3},{3,2},{4,5},{5,4},{6,7},{7,6},{8,9},{9,8},{10,11... | collective-permute-start | bytes 786440 | tf_op jit(solution)/shard_map/ppermute | solution.py:190
  51.4 12.2 %collective-permute-start.5 = (bf16[512,256]{1,0:T(8,128)(2,1)S(1)}, bf16[512,256]{1,0:T(8,128)(2,1)S(1)}, u32[]{:S(2)}, u32[]{:S(2)}) collective-permute-start(bf16[512,256]{1,0:T(8,128)(2,1)S(1)} %collective-permute-done.1.b0), channel_id=1, source_target_pairs={{0,3},{1,2},{2,1},{3,0},{4,7},{5,6},{6,5},{7,4},{8,11},{9,10},{10,... | collective-permute-start | bytes 786440 | tf_op jit(solution)/shard_map/ppermute | solution.py:190
  53.3 9.8 %collective-permute-start.4 = (bf16[512,256]{1,0:T(8,128)(2,1)S(1)}, bf16[512,256]{1,0:T(8,128)(2,1)S(1)}, u32[]{:S(2)}, u32[]{:S(2)}) collective-permute-start(bf16[512,256]{1,0:T(8,128)(2,1)S(1)} %collective-permute-done.3.b2), channel_id=1, source_target_pairs={{0,4},{1,5},{2,6},{3,7},{4,0},{5,1},{6,2},{7,3},{8,12},{9,13},{10,... | collective-permute-start | bytes 786440 | tf_op jit(solution)/shard_map/ppermute | solution.py:190
  66.6 4.8 %collective-permute-start.9 = (bf16[128,4096]{1,0:T(8,128)(2,1)S(1)}, bf16[128,4096]{1,0:T(8,128)(2,1)S(1)}, u32[]{:S(2)}, u32[]{:S(2)}) collective-permute-start(bf16[128,4096]{1,0:T(8,128)(2,1)S(1)} %get-tuple-element.21), channel_id=1, source_target_pairs={{0,8},{8,0},{16,24},{24,16},{32,40},{40,32},{48,56},{56,48},{64,72... | collective-permute-start | bytes 3145736 | tf_op jit(solution)/shard_map/ppermute | solution.py:287
  71.3 5.9 %collective-permute-start.8 = (bf16[128,4096]{1,0:T(8,128)(2,1)S(1)}, bf16[128,4096]{1,0:T(8,128)(2,1)S(1)}, u32[]{:S(2)}, u32[]{:S(2)}) collective-permute-start(bf16[128,4096]{1,0:T(8,128)(2,1)S(1)} %get-tuple-element.19), channel_id=1, source_target_pairs={{0,8},{8,0},{16,24},{24,16},{32,40},{40,32},{48,56},{56,48},{64,72... | collective-permute-start | bytes 3145736 | tf_op jit(solution)/shard_map/ppermute | solution.py:290
  71.7 28.4 %collective-permute-start.10 = (bf16[64,4096]{1,0:T(8,128)(2,1)S(1)}, bf16[64,4096]{1,0:T(8,128)(2,1)S(1)}, u32[]{:S(2)}, u32[]{:S(2)}) collective-permute-start(bf16[64,4096]{1,0:T(8,128)(2,1)S(1)} %get-tuple-element.29), channel_id=1, source_target_pairs={{0,80},{8,120},{16,64},{24,104},{32,112},{40,88},{48,96},{56,72},{... | collective-permute-start | bytes 1572872 | tf_op jit(solution)/shard_map/ppermute | solution.py:283
  75.6 24.5 %collective-permute-start.11 = (bf16[64,4096]{1,0:T(8,128)(2,1)S(1)}, bf16[64,4096]{1,0:T(8,128)(2,1)S(1)}, u32[]{:S(2)}, u32[]{:S(2)}) collective-permute-start(bf16[64,4096]{1,0:T(8,128)(2,1)S(1)} %get-tuple-element.30), channel_id=1, source_target_pairs={{0,32},{8,104},{16,48},{24,120},{32,0},{40,72},{48,16},{56,88},{64... | collective-permute-start | bytes 1572872 | tf_op jit(solution)/shard_map/ppermute | solution.py:283
  77.6 22.5 %collective-permute-start.12 = (bf16[32,4096]{1,0:T(8,128)(2,1)S(1)}, bf16[32,4096]{1,0:T(8,128)(2,1)S(1)}, u32[]{:S(2)}, u32[]{:S(2)}) collective-permute-start(bf16[32,4096]{1,0:T(8,128)(2,1)S(1)} %slice.53), channel_id=1, source_target_pairs={{0,64},{8,72},{16,80},{24,88},{32,96},{40,104},{48,112},{56,120},{... | collective-permute-start | bytes 786440 | tf_op jit(solution)/shard_map/ppermute | solution.py:283
  79.9 20.9 %collective-permute-start.13 = (bf16[64,4096]{1,0:T(8,128)(2,1)S(1)}, bf16[64,4096]{1,0:T(8,128)(2,1)S(1)}, u32[]{:S(2)}, u32[]{:S(2)}) collective-permute-start(bf16[64,4096]{1,0:T(8,128)(2,1)S(1)} %slice.56), channel_id=1, source_target_pairs={{0,16},{8,56},{16,0},{24,40},{32,48},{40,24},{48,32},{56,8},{64,80... | collective-permute-start | bytes 1572872 | tf_op jit(solution)/shard_map/ppermute | solution.py:283
  100.9 2.0 %collective-permute-start.14 = (f32[32,4096]{1,0:T(8,128)S(1)}, f32[32,4096]{1,0:T(8,128)S(1)}, u32[]{:S(2)}, u32[]{:S(2)}) collective-permute-start(f32[32,4096]{1,0:T(8,128)S(1)} %convert_add_fusion.1), channel_id=1, source_target_pairs={{0,8},{8,0},{16,24},{24,16},{32,40},{40,32},{48,56},{56,48},{64,72... | collective-permute-start | bytes 1572872 | tf_op jit(solution)/shard_map/ppermute | solution.py:297

commit v5 on v4

--- a/solution.py
+++ b/solution.py
@@ -17,7 +17,7 @@
 VMEM = pl.BlockSpec(memory_space=pltpu.VMEM)
 HBM = pl.BlockSpec(memory_space=pltpu.HBM)
 
-SLOTS = ((5, 7), (2, 6), (1, 3), (4, 4))
+SLOTS = ((5, 7), (4, 4), (2, 6), (1, 3))
 
 
 def call(kernel, out_shape, n_scalars, n_arrays, scratch=(), flops=0, moved=0, limit=8):
@@ -95,11 +95,11 @@
     within = row % 128
     sender = place_ref[1] ^ ((row // 128) % 2)
     first = chunk == 0
-    paired = first | (within < 64)
+    paired = ~first | (within < 64)
     slot = jnp.where(
         first,
-        jnp.where(within < 64, 5 + 2 * sender, 2 + 4 * sender),
-        jnp.where(within < 64, 1 + 2 * sender, jnp.where(within < 96, 4, 0)),
+        jnp.where(within < 64, 5 + 2 * sender, jnp.where(within < 96, 4, 0)),
+        jnp.where(within < 64, 2 + 4 * sender, 1 + 2 * sender),
     )
     core = jnp.where(paired, sender ^ ((within // 32) % 2), sender)
     j = (place_ref[0] ^ slot) * 8 + core * 4 + (within % 32) // BW
@@ -286,15 +286,15 @@
     kept_b, sent_b = far(rows // 2)
     sums_a = kept_a + lax.ppermute(sent_a, "kc", swap).astype(F32)
     got0 = to_slot(sums_a[: 2 * share].astype(BF16), SLOTS[0])
-    got1 = to_slot(sums_a[2 * share :].astype(BF16), SLOTS[1])
+    got1 = to_slot(sums_a[2 * share : 3 * share].astype(BF16), SLOTS[1])
     sums_b = kept_b + lax.ppermute(sent_b, "kc", swap).astype(F32)
     got2 = to_slot(sums_b[: 2 * share].astype(BF16), SLOTS[2])
-    got3 = to_slot(sums_b[2 * share : 3 * share].astype(BF16), SLOTS[3])
-    mine = sums_b[3 * share :] + got0[:share].astype(F32) + got1[:share].astype(F32) + got3.astype(F32)
-    other = got0[share:].astype(F32) + got1[share:].astype(F32)
-    mine, other, got2 = lax.optimization_barrier((mine, other, got2))
-    other = other + got2[share:].astype(F32)
-    return (mine + got2[:share].astype(F32) + lax.ppermute(other, "kc", swap)).T
+    got3 = to_slot(sums_b[2 * share :].astype(BF16), SLOTS[3])
+    mine = sums_a[3 * share :] + got0[:share].astype(F32) + got1.astype(F32) + got2[:share].astype(F32)
+    other = got0[share:].astype(F32) + got2[share:].astype(F32)
+    mine, other, got3 = lax.optimization_barrier((mine, other, got3))
+    other = other + got3[share:].astype(F32)
+    return (mine + got3[:share].astype(F32) + lax.ppermute(other, "kc", swap)).T
 
 
 def solution(mesh):

time: 104 us -> 105 us (level)
  starting transfers between devices: 28.1 us -> 29.2 us
where the time goes in v5:
time: 105 us; the launch traced here: 104 us
  waiting for transfers between devices  44.7 us (43%)
  starting transfers between devices  29.2 us (28%)
  Pallas kernels  25.3 us (24%)
  local copies, waits for them, and re-layouts  3.4 us (3%)
  other arithmetic  1.67 us (2%)
    ppermute x4, waiting for transfers between devices, to_slot(): return lax.ppermute(array, 'kc', pairs)  20.1 us
    all_to_all x1, waiting for transfers between devices, per_device(): factors = lax.all_to_all(payload, 'kc', 0, 0, axis_index_groups=same_core)  18.7 us
    ppermute x4, starting transfers between devices, to_slot(): return lax.ppermute(array, 'kc', pairs)  8.73 us
    all_to_all x1, starting transfers between devices, per_device(): factors = lax.all_to_all(payload, 'kc', 0, 0, axis_index_groups=same_core)  8.34 us
    pallas_call x2, Pallas kernels, columns(): pl.pallas_call(functools.partial(columns_kernel, far), out_shape=jax.Shap...  8.26 us
    ppermute x7, starting transfers between devices, over_ia(): return lax.ppermute(array, 'ia', [(i, i ^ bits) for i in range(ia_size)])  8.07 us
    pallas_call x2, Pallas kernels, far(): call(functools.partial(far_kernel, tile, lo), (jax.ShapeDtypeStruct((part...  5.95 us
    pallas_call x1, Pallas kernels, per_device(): call(functools.partial(near_kernel, tile), jax.ShapeDtypeStruct((rows, lo...  5.17 us
  transfers between devices with their start and end apart: 16, of which 8 were waited for; matrix products, arithmetic and copies ran while one was open for 1% of the time, Pallas kernels for 17%

profile of v5, /device:TPU:1, one launch (start us, length us, event | category | flops | bytes accessed | tf_op | source)
XLA Modules:
  0.0 104.4 jit_solution(11892801990200410718)
XLA Ops:
  0.0 2.5 %shard_map.37 = bf16[8,256,512]{2,1,0:T(8,128)(2,1)} custom-call(bf16[128,4096]{1,0:T(8,128)(2,1)} %occupied_ref.1, bf16[128,512]{1,0:T(8,128)(2,1)} %virtual_ref.1), custom_call_target="tpu_custom_call" | custom-call | bytes 4194304 | tf_op jit(solution)/shard_map/pallas_call | solution.py:192
  2.5 8.3 %all-to-all-start = ((bf16[8,256,512]{2,1,0:T(8,128)(2,1)}), bf16[8,256,512]{2,1,0:T(8,128)(2,1)S(1)}, u32[]{:S(2)}, u32[]{:S(2)}) async-start(bf16[8,256,512]{2,1,0:T(8,128)(2,1)} %shard_map.37), calls=%async_computation | async-start | bytes 4194304 | tf_op jit(solution)/shard_map/all_to_all | solution.py:205
  10.9 0.1 pad_add_fusion.place_ref
  11.0 4.1 %shard_map.38.amplitudes_ref = bf16[4096,1024]{1,0:T(8,128)(2,1)S(1)} custom-call(s32[4]{0:T(128)S(1)} %pad_add_fusion.place_ref, bf16[4096,2048]{1,0:T(8,128)(2,1)} %amplitudes_ref.3), custom_call_target="tpu_custom_call" | custom-call | bytes 16777216 | tf_op jit(solution)/shard_map/pallas_call | solution.py:207
  15.1 3.3 %copy-done = bf16[4096,1024]{1,0:T(8,128)(2,1)} copy-done((bf16[4096,1024]{1,0:T(8,128)(2,1)}, bf16[4096,1024]{1,0:T(8,128)(2,1)S(1)}, u32[]{:S(2)}) %copy-start) | copy-done | bytes 8388632
  18.4 18.7 %all-to-all-done.factors_ref = bf16[8,256,512]{2,1,0:T(8,128)(2,1)S(1)} async-done(((bf16[8,256,512]{2,1,0:T(8,128)(2,1)}), bf16[8,256,512]{2,1,0:T(8,128)(2,1)S(1)}, u32[]{:S(2)}, u32[]{:S(2)}) %all-to-all-start) | async-done | bytes 2097184 | tf_op jit(solution)/shard_map/all_to_all | solution.py:205
  37.0 1.0 shard_map.40
  38.0 1.3 %collective-permute-start = (f32[256,512]{1,0:T(8,128)S(1)}, f32[256,512]{1,0:T(8,128)S(1)}, u32[]{:S(2)}, u32[]{:S(2)}) collective-permute-start(f32[256,512]{1,0:T(8,128)S(1)} %shard_map.40), channel_id=1, source_target_pairs={{0,8},{8,0},{16,24},{24,16},{32,40},{40,32},{48,56},{56,48},{64,72... | collective-permute-start | bytes 1572872 | tf_op jit(solution)/shard_map/ppermute | solution.py:231
  39.3 1.0 shard_map.39.kept_ref
  40.4 0.5 collective-permute-done.came_ref
  40.9 1.4 %shard_map.41.b0 = bf16[512,256]{1,0:T(8,128)(2,1)S(1)} custom-call(s32[4]{0:T(128)S(1)} %pad_add_fusion.place_ref, f32[256,512]{1,0:T(8,128)S(1)} %shard_map.39.kept_ref, f32[256,512]{1,0:T(8,128)S(1)} %collective-permute-done.came_ref), custom_call_target="tpu_custom_call" | custom-call | flops 268435456 | bytes 2097152 | tf_op jit(solution)/shard_map/pallas_call | solution.py:232
  42.3 0.0 slice-start.1
  42.3 0.4 collective-permute-start.1
  42.7 2.9 %collective-permute-start.3 = (bf16[512,256]{1,0:T(8,128)(2,1)S(1)}, bf16[512,256]{1,0:T(8,128)(2,1)S(1)}, u32[]{:S(2)}, u32[]{:S(2)}) collective-permute-start(bf16[512,256]{1,0:T(8,128)(2,1)S(1)} %shard_map.41.b0), channel_id=1, source_target_pairs={{0,2},{1,3},{2,0},{3,1},{4,6},{5,7},{6,4},{7,5},{8,10},{9,11},{10,... | collective-permute-start | bytes 786440 | tf_op jit(solution)/shard_map/ppermute | solution.py:190
  45.6 0.4 collective-permute-start.6
  46.0 0.4 collective-permute-start.7
  46.3 4.1 %shard_map.42.held_ref = bf16[4096,1024]{1,0:T(8,128)(2,1)S(1)} custom-call(s32[4]{0:T(128)S(1)} %pad_add_fusion.place_ref, bf16[4096,2048]{1,0:T(8,128)(2,1)} %amplitudes_ref.3), custom_call_target="tpu_custom_call" | custom-call | bytes 16777216 | tf_op jit(solution)/shard_map/pallas_call | solution.py:207
  50.5 0.0 collective-permute-done.1.b0
  50.5 0.9 collective-permute-start.2
  51.4 1.9 %collective-permute-start.5 = (bf16[512,256]{1,0:T(8,128)(2,1)S(1)}, bf16[512,256]{1,0:T(8,128)(2,1)S(1)}, u32[]{:S(2)}, u32[]{:S(2)}) collective-permute-start(bf16[512,256]{1,0:T(8,128)(2,1)S(1)} %collective-permute-done.1.b0), channel_id=1, source_target_pairs={{0,3},{1,2},{2,1},{3,0},{4,7},{5,6},{6,5},{7,4},{8,11},{9,10},{10,... | collective-permute-start | bytes 786440 | tf_op jit(solution)/shard_map/ppermute | solution.py:190
  53.3 0.0 collective-permute-done.3.b2
  53.3 1.1 %collective-permute-start.4 = (bf16[512,256]{1,0:T(8,128)(2,1)S(1)}, bf16[512,256]{1,0:T(8,128)(2,1)S(1)}, u32[]{:S(2)}, u32[]{:S(2)}) collective-permute-start(bf16[512,256]{1,0:T(8,128)(2,1)S(1)} %collective-permute-done.3.b2), channel_id=1, source_target_pairs={{0,4},{1,5},{2,6},{3,7},{4,0},{5,1},{6,2},{7,3},{8,12},{9,13},{10,... | collective-permute-start | bytes 786440 | tf_op jit(solution)/shard_map/ppermute | solution.py:190
  54.5 2.9 %collective-permute-done.6.b1 = bf16[512,256]{1,0:T(8,128)(2,1)S(1)} collective-permute-done((bf16[512,256]{1,0:T(8,128)(2,1)S(1)}, bf16[512,256]{1,0:T(8,128)(2,1)S(1)}, u32[]{:S(2)}, u32[]{:S(2)}) %collective-permute-start.6) | collective-permute-done | bytes 262176 | tf_op jit(solution)/shard_map/ppermute | solution.py:190
  57.4 0.6 collective-permute-done.7.b3
  58.0 5.2 %shard_map.43.near_ref = f32[512,4096]{1,0:T(8,128)S(1)} custom-call(s32[4]{0:T(128)S(1)} %pad_add_fusion.place_ref, bf16[512,256]{1,0:T(8,128)(2,1)S(1)} %shard_map.41.b0, bf16[512,256]{1,0:T(8,128)(2,1)S(1)} %collective-permute-done.6.b1, bf16[512,256]{1,0:T(8,128)(2,1)S(1)} %collective-permute-done.3.b2, bf16[512,256]{1,0:T(8,128)(2,1)S(1)} %collective-permute-done.7.b3, ...), custom_call_target="tpu_custom_call" | custom-call | flops 4294967296 | bytes 17825792 | tf_op jit(solution)/shard_map/pallas_call | solution.py:253
  63.2 0.0 collective-permute-done.2.b1
  63.2 0.0 collective-permute-done.4.b2
  63.2 0.4 collective-permute-done.5.b3
  63.6 3.0 %shard_map.44 = (f32[128,4096]{1,0:T(8,128)S(1)}, bf16[128,4096]{1,0:T(8,128)(2,1)S(1)}) custom-call(s32[4]{0:T(128)S(1)} %pad_add_fusion.place_ref, bf16[512,256]{1,0:T(8,128)(2,1)S(1)} %collective-permute-done.1.b0, bf16[512,256]{1,0:T(8,128)(2,1)S(1)} %collective-permute-done.2.b1, bf16[512,256]{1,0:T(8,128)(2,1)S(1)} %collective-permute-done.4.b2, ...), custom_call_target="tpu_custom_call" | custom-call | flops 2147483648 | bytes 12582912 | tf_op jit(solution)/shard_map/pallas_call | solution.py:265
  66.6 1.7 %collective-permute-start.8 = (bf16[128,4096]{1,0:T(8,128)(2,1)S(1)}, bf16[128,4096]{1,0:T(8,128)(2,1)S(1)}, u32[]{:S(2)}, u32[]{:S(2)}) collective-permute-start(bf16[128,4096]{1,0:T(8,128)(2,1)S(1)} %get-tuple-element.19), channel_id=1, source_target_pairs={{0,8},{8,0},{16,24},{24,16},{32,40},{40,32},{48,56},{56,48},{64,72... | collective-permute-start | bytes 3145736 | tf_op jit(solution)/shard_map/ppermute | solution.py:287
  68.3 3.0 %shard_map.45 = (f32[128,4096]{1,0:T(8,128)S(1)}, bf16[128,4096]{1,0:T(8,128)(2,1)S(1)}) custom-call(s32[4]{0:T(128)S(1)} %pad_add_fusion.place_ref, bf16[512,256]{1,0:T(8,128)(2,1)S(1)} %collective-permute-done.1.b0, bf16[512,256]{1,0:T(8,128)(2,1)S(1)} %collective-permute-done.2.b1, bf16[512,256]{1,0:T(8,128)(2,1)S(1)} %collective-permute-done.4.b2, ...), custom_call_target="tpu_custom_call" | custom-call | flops 2147483648 | bytes 12582912 | tf_op jit(solution)/shard_map/pallas_call | solution.py:265
  71.3 0.1 collective-permute-start.11
  71.4 0.0 collective-permute-done.8
  71.4 0.3 fusion.2
  71.8 3.9 %collective-permute-start.9 = (bf16[64,4096]{1,0:T(8,128)(2,1)S(1)}, bf16[64,4096]{1,0:T(8,128)(2,1)S(1)}, u32[]{:S(2)}, u32[]{:S(2)}) collective-permute-start(bf16[64,4096]{1,0:T(8,128)(2,1)S(1)} %slice.49), channel_id=1, source_target_pairs={{0,80},{8,120},{16,64},{24,104},{32,112},{40,88},{48,96},{56,72},{... | collective-permute-start | bytes 1572872 | tf_op jit(solution)/shard_map/ppermute | solution.py:283
  75.7 0.0 collective-permute-done.11
  75.7 0.2 add_convert_fusion
  75.9 0.1 fusion.3
  76.0 1.7 %collective-permute-start.12 = (bf16[64,4096]{1,0:T(8,128)(2,1)S(1)}, bf16[64,4096]{1,0:T(8,128)(2,1)S(1)}, u32[]{:S(2)}, u32[]{:S(2)}) collective-permute-start(bf16[64,4096]{1,0:T(8,128)(2,1)S(1)} %get-tuple-element.28), channel_id=1, source_target_pairs={{0,32},{8,104},{16,48},{24,120},{32,0},{40,72},{48,16},{56,88},{64... | collective-permute-start | bytes 1572872 | tf_op jit(solution)/shard_map/ppermute | solution.py:283
  77.7 2.3 %collective-permute-start.10 = (bf16[32,4096]{1,0:T(8,128)(2,1)S(1)}, bf16[32,4096]{1,0:T(8,128)(2,1)S(1)}, u32[]{:S(2)}, u32[]{:S(2)}) collective-permute-start(bf16[32,4096]{1,0:T(8,128)(2,1)S(1)} %slice.51), channel_id=1, source_target_pairs={{0,64},{8,72},{16,80},{24,88},{32,96},{40,104},{48,112},{56,120},{... | collective-permute-start | bytes 786440 | tf_op jit(solution)/shard_map/ppermute | solution.py:283
  80.0 0.8 collective-permute-start.13
  80.8 19.4 %collective-permute-done.10 = bf16[32,4096]{1,0:T(8,128)(2,1)S(1)} collective-permute-done((bf16[32,4096]{1,0:T(8,128)(2,1)S(1)}, bf16[32,4096]{1,0:T(8,128)(2,1)S(1)}, u32[]{:S(2)}, u32[]{:S(2)}) %collective-permute-start.10) | collective-permute-done | bytes 262176 | tf_op jit(solution)/shard_map/ppermute | solution.py:283
  100.2 0.0 collective-permute-done.9
  100.2 0.2 convert_add_fusion.2
  100.4 0.7 collective-permute-done.13
  101.1 0.9 collective-permute-start.14
  102.0 1.5 %collective-permute-done.14 = f32[32,4096]{1,0:T(8,128)S(1)} collective-permute-done((f32[32,4096]{1,0:T(8,128)S(1)}, f32[32,4096]{1,0:T(8,128)S(1)}, u32[]{:S(2)}, u32[]{:S(2)}) %collective-permute-start.14) | collective-permute-done | bytes 524320 | tf_op jit(solution)/shard_map/ppermute | solution.py:297
  103.6 0.9 add_bitcast_fusion
  (9 shorter events, 0.1 us)
Async XLA Ops:
  2.5 34.5 %all-to-all-start = ((bf16[8,256,512]{2,1,0:T(8,128)(2,1)}), bf16[8,256,512]{2,1,0:T(8,128)(2,1)S(1)}, u32[]{:S(2)}, u32[]{:S(2)}) async-start(bf16[8,256,512]{2,1,0:T(8,128)(2,1)} %shard_map.37), calls=%async_computation | async-start | bytes 4194304 | tf_op jit(solution)/shard_map/all_to_all | solution.py:205
  15.1 3.3 %copy-start = (bf16[4096,1024]{1,0:T(8,128)(2,1)}, bf16[4096,1024]{1,0:T(8,128)(2,1)S(1)}, u32[]{:S(2)}) copy-start(bf16[4096,1024]{1,0:T(8,128)(2,1)S(1)} %shard_map.38.amplitudes_ref) | copy-start | bytes 25165828
  38.0 2.9 %collective-permute-start = (f32[256,512]{1,0:T(8,128)S(1)}, f32[256,512]{1,0:T(8,128)S(1)}, u32[]{:S(2)}, u32[]{:S(2)}) collective-permute-start(f32[256,512]{1,0:T(8,128)S(1)} %shard_map.40), channel_id=1, source_target_pairs={{0,8},{8,0},{16,24},{24,16},{32,40},{40,32},{48,56},{56,48},{64,72... | collective-permute-start | bytes 1572872 | tf_op jit(solution)/shard_map/ppermute | solution.py:231
  40.9 22.7 %slice-start = ((s8[8388608]{0:T(1024)(128)(4,1)}), s8[4194304]{0:T(1024)(128)(4,1)S(1)}, s32[]{:S(2)}) async-start(s8[8388608]{0:T(1024)(128)(4,1)} %bitcast.6), calls=%async_computation.1 | async-start | bytes 8388608
  42.3 21.4 %slice-start.1 = ((s8[8388608]{0:T(1024)(128)(4,1)}), s8[4194304]{0:T(1024)(128)(4,1)S(1)}, s32[]{:S(2)}) async-start(s8[8388608]{0:T(1024)(128)(4,1)} %bitcast.6), calls=%async_computation.2 | async-start | bytes 8388608
  42.3 8.2 %collective-permute-start.1 = (bf16[512,256]{1,0:T(8,128)(2,1)S(1)}, bf16[512,256]{1,0:T(8,128)(2,1)S(1)}, u32[]{:S(2)}, u32[]{:S(2)}) collective-permute-start(bf16[512,256]{1,0:T(8,128)(2,1)S(1)} %shard_map.41.b0), channel_id=1, source_target_pairs={{0,4},{1,5},{2,6},{3,7},{4,0},{5,1},{6,2},{7,3},{8,12},{9,13},{10,... | collective-permute-start | bytes 786440 | tf_op jit(solution)/shard_map/ppermute | solution.py:190
  42.7 10.7 %collective-permute-start.3 = (bf16[512,256]{1,0:T(8,128)(2,1)S(1)}, bf16[512,256]{1,0:T(8,128)(2,1)S(1)}, u32[]{:S(2)}, u32[]{:S(2)}) collective-permute-start(bf16[512,256]{1,0:T(8,128)(2,1)S(1)} %shard_map.41.b0), channel_id=1, source_target_pairs={{0,2},{1,3},{2,0},{3,1},{4,6},{5,7},{6,4},{7,5},{8,10},{9,11},{10,... | collective-permute-start | bytes 786440 | tf_op jit(solution)/shard_map/ppermute | solution.py:190
  45.6 11.8 %collective-permute-start.6 = (bf16[512,256]{1,0:T(8,128)(2,1)S(1)}, bf16[512,256]{1,0:T(8,128)(2,1)S(1)}, u32[]{:S(2)}, u32[]{:S(2)}) collective-permute-start(bf16[512,256]{1,0:T(8,128)(2,1)S(1)} %shard_map.41.b0), channel_id=1, source_target_pairs={{0,1},{1,0},{2,3},{3,2},{4,5},{5,4},{6,7},{7,6},{8,9},{9,8},{10,11... | collective-permute-start | bytes 786440 | tf_op jit(solution)/shard_map/ppermute | solution.py:190
  46.0 12.0 %collective-permute-start.7 = (bf16[512,256]{1,0:T(8,128)(2,1)S(1)}, bf16[512,256]{1,0:T(8,128)(2,1)S(1)}, u32[]{:S(2)}, u32[]{:S(2)}) collective-permute-start(bf16[512,256]{1,0:T(8,128)(2,1)S(1)} %shard_map.41.b0), channel_id=1, source_target_pairs={{0,3},{1,2},{2,1},{3,0},{4,7},{5,6},{6,5},{7,4},{8,11},{9,10},{10,... | collective-permute-start | bytes 786440 | tf_op jit(solution)/shard_map/ppermute | solution.py:190
  50.5 12.7 %collective-permute-start.2 = (bf16[512,256]{1,0:T(8,128)(2,1)S(1)}, bf16[512,256]{1,0:T(8,128)(2,1)S(1)}, u32[]{:S(2)}, u32[]{:S(2)}) collective-permute-start(bf16[512,256]{1,0:T(8,128)(2,1)S(1)} %collective-permute-done.1.b0), channel_id=1, source_target_pairs={{0,1},{1,0},{2,3},{3,2},{4,5},{5,4},{6,7},{7,6},{8,9},{9,8},{10,11... | collective-permute-start | bytes 786440 | tf_op jit(solution)/shard_map/ppermute | solution.py:190
  51.4 12.2 %collective-permute-start.5 = (bf16[512,256]{1,0:T(8,128)(2,1)S(1)}, bf16[512,256]{1,0:T(8,128)(2,1)S(1)}, u32[]{:S(2)}, u32[]{:S(2)}) collective-permute-start(bf16[512,256]{1,0:T(8,128)(2,1)S(1)} %collective-permute-done.1.b0), channel_id=1, source_target_pairs={{0,3},{1,2},{2,1},{3,0},{4,7},{5,6},{6,5},{7,4},{8,11},{9,10},{10,... | collective-permute-start | bytes 786440 | tf_op jit(solution)/shard_map/ppermute | solution.py:190
  53.3 9.8 %collective-permute-start.4 = (bf16[512,256]{1,0:T(8,128)(2,1)S(1)}, bf16[512,256]{1,0:T(8,128)(2,1)S(1)}, u32[]{:S(2)}, u32[]{:S(2)}) collective-permute-start(bf16[512,256]{1,0:T(8,128)(2,1)S(1)} %collective-permute-done.3.b2), channel_id=1, source_target_pairs={{0,4},{1,5},{2,6},{3,7},{4,0},{5,1},{6,2},{7,3},{8,12},{9,13},{10,... | collective-permute-start | bytes 786440 | tf_op jit(solution)/shard_map/ppermute | solution.py:190
  66.6 4.8 %collective-permute-start.8 = (bf16[128,4096]{1,0:T(8,128)(2,1)S(1)}, bf16[128,4096]{1,0:T(8,128)(2,1)S(1)}, u32[]{:S(2)}, u32[]{:S(2)}) collective-permute-start(bf16[128,4096]{1,0:T(8,128)(2,1)S(1)} %get-tuple-element.19), channel_id=1, source_target_pairs={{0,8},{8,0},{16,24},{24,16},{32,40},{40,32},{48,56},{56,48},{64,72... | collective-permute-start | bytes 3145736 | tf_op jit(solution)/shard_map/ppermute | solution.py:287
  71.3 4.4 %collective-permute-start.11 = (bf16[128,4096]{1,0:T(8,128)(2,1)S(1)}, bf16[128,4096]{1,0:T(8,128)(2,1)S(1)}, u32[]{:S(2)}, u32[]{:S(2)}) collective-permute-start(bf16[128,4096]{1,0:T(8,128)(2,1)S(1)} %get-tuple-element.21), channel_id=1, source_target_pairs={{0,8},{8,0},{16,24},{24,16},{32,40},{40,32},{48,56},{56,48},{64,72... | collective-permute-start | bytes 3145736 | tf_op jit(solution)/shard_map/ppermute | solution.py:290
  71.8 28.4 %collective-permute-start.9 = (bf16[64,4096]{1,0:T(8,128)(2,1)S(1)}, bf16[64,4096]{1,0:T(8,128)(2,1)S(1)}, u32[]{:S(2)}, u32[]{:S(2)}) collective-permute-start(bf16[64,4096]{1,0:T(8,128)(2,1)S(1)} %slice.49), channel_id=1, source_target_pairs={{0,80},{8,120},{16,64},{24,104},{32,112},{40,88},{48,96},{56,72},{... | collective-permute-start | bytes 1572872 | tf_op jit(solution)/shard_map/ppermute | solution.py:283
  76.0 24.2 %collective-permute-start.12 = (bf16[64,4096]{1,0:T(8,128)(2,1)S(1)}, bf16[64,4096]{1,0:T(8,128)(2,1)S(1)}, u32[]{:S(2)}, u32[]{:S(2)}) collective-permute-start(bf16[64,4096]{1,0:T(8,128)(2,1)S(1)} %get-tuple-element.28), channel_id=1, source_target_pairs={{0,32},{8,104},{16,48},{24,120},{32,0},{40,72},{48,16},{56,88},{64... | collective-permute-start | bytes 1572872 | tf_op jit(solution)/shard_map/ppermute | solution.py:283
  77.7 22.5 %collective-permute-start.10 = (bf16[32,4096]{1,0:T(8,128)(2,1)S(1)}, bf16[32,4096]{1,0:T(8,128)(2,1)S(1)}, u32[]{:S(2)}, u32[]{:S(2)}) collective-permute-start(bf16[32,4096]{1,0:T(8,128)(2,1)S(1)} %slice.51), channel_id=1, source_target_pairs={{0,64},{8,72},{16,80},{24,88},{32,96},{40,104},{48,112},{56,120},{... | collective-permute-start | bytes 786440 | tf_op jit(solution)/shard_map/ppermute | solution.py:283
  80.0 21.1 %collective-permute-start.13 = (bf16[64,4096]{1,0:T(8,128)(2,1)S(1)}, bf16[64,4096]{1,0:T(8,128)(2,1)S(1)}, u32[]{:S(2)}, u32[]{:S(2)}) collective-permute-start(bf16[64,4096]{1,0:T(8,128)(2,1)S(1)} %get-tuple-element.27), channel_id=1, source_target_pairs={{0,16},{8,56},{16,0},{24,40},{32,48},{40,24},{48,32},{56,8},{64,80... | collective-permute-start | bytes 1572872 | tf_op jit(solution)/shard_map/ppermute | solution.py:283
  101.1 2.5 %collective-permute-start.14 = (f32[32,4096]{1,0:T(8,128)S(1)}, f32[32,4096]{1,0:T(8,128)S(1)}, u32[]{:S(2)}, u32[]{:S(2)}) collective-permute-start(f32[32,4096]{1,0:T(8,128)S(1)} %convert_add_fusion.1), channel_id=1, source_target_pairs={{0,8},{8,0},{16,24},{24,16},{32,40},{40,32},{48,56},{56,48},{64,72... | collective-permute-start | bytes 1572872 | tf_op jit(solution)/shard_map/ppermute | solution.py:297
